TPU v7x, 128 devices: a whole 4x4x4 slice. The times are simulated.
128 devices in a mesh: node: 8 (over z, core), local: 16 (over x, y).
Axes of the slice: x: 4, y: 4, z: 4, core: 2. Of those that a mesh axis runs over, the one named last changes fastest.
Arguments:
- patches: bfloat16 [1024, 1408], P('node'), may hold values from -6 to 6
- norm_gain: float32 [1408], replicated, may hold values from 0.25 to 1.75
- vit_up: bfloat16 [1408, 5632], P(None, 'local'), may hold values from -0.15625 to 0.15625
- vit_down: bfloat16 [5632, 1408], P('local'), may hold values from -0.078125 to 0.078125
- adapter: bfloat16 [1408, 5120], P('local'), may hold values from -0.15625 to 0.15625
- text_rows: bfloat16 [15360, 5120], P(('node', 'local')), may hold values from -6 to 6
- router: bfloat16 [5120, 8], replicated, may hold values from -0.15625 to 0.15625
- expert_ids: int32 [16384, 1], P(('node', 'local')), may hold values from 0 to 7
- w_gate: bfloat16 [8, 5120, 4096], P('node', None, 'local'), may hold values from -0.15625 to 0.15625
- w_up: bfloat16 [8, 5120, 4096], P('node', None, 'local'), may hold values from -0.15625 to 0.15625
- w_down: bfloat16 [8, 4096, 5120], P('node', 'local'), may hold values from -0.25 to 0.25
Outputs:
- expert_out: bfloat16 [8, 1792, 5120], P('node', 'local')
All inputs are finite; a program needn't handle non-finite values.
Results may differ from a plain program's by a relative error of at most 0.029.
Values may be sent and summed in bfloat16 or wider, within the bound.
A program may use at most 128 MiB of HBM per device.

v0:
```python
import jax
import jax.numpy as jnp
from jax import lax
from jax.sharding import PartitionSpec as P


def layer_norm(rows, gain):
    values = rows.astype(jnp.float32)
    center = jnp.mean(values, axis=-1, keepdims=True)
    spread = jnp.mean((values - center) ** 2, axis=-1, keepdims=True)
    return (values - center) * lax.rsqrt(spread + 1e-05) * gain


def on_device(
    patches,
    norm_gain,
    vit_up,
    vit_down,
    adapter,
    text_rows,
    router,
    expert_ids,
    w_gate,
    w_up,
    w_down,
):
    member = lax.axis_index("local")
    normed = layer_norm(patches, norm_gain).astype(jnp.bfloat16)
    inner = jax.nn.gelu(
        jnp.dot(normed, vit_up, preferred_element_type=jnp.float32), approximate=True
    ).astype(jnp.bfloat16)
    partial_sum = jnp.dot(inner, vit_down, preferred_element_type=jnp.float32)
    feature_block = adapter.shape[0]
    total = lax.psum(partial_sum.astype(jnp.bfloat16), "local").astype(jnp.float32)
    vision = (patches.astype(jnp.float32) + total).astype(jnp.bfloat16)
    own_block = lax.dynamic_slice_in_dim(vision, member * feature_block, feature_block, 1)
    picked = own_block
    embed = lax.psum_scatter(
        jnp.dot(picked, adapter, preferred_element_type=jnp.float32).astype(jnp.bfloat16),
        "local",
        scatter_dimension=0,
        tiled=True,
    )
    seq = jnp.concatenate([text_rows, embed], axis=0)
    row_count = seq.shape[0]
    expert_count = router.shape[1]
    capacity = 7 * row_count // (8 * lax.axis_size("node"))
    logits = jnp.dot(seq, router, preferred_element_type=jnp.float32)
    chosen = expert_ids[:, 0]
    table = (chosen[:, None] == jnp.arange(expert_count, dtype=jnp.int32)[None, :]).astype(
        jnp.int32
    )
    score = jax.nn.sigmoid(jnp.sum(logits * table.astype(jnp.float32), axis=1))
    scaled = (seq.astype(jnp.float32) * score[:, None]).astype(jnp.bfloat16)
    rank = jnp.sum((jnp.cumsum(table, axis=0) - 1) * table, axis=1)
    slot = chosen * capacity + rank
    place = (
        (slot[None, :] == jnp.arange(expert_count * capacity, dtype=jnp.int32)[:, None])
        & (rank < capacity)[None, :]
    ).astype(jnp.bfloat16)
    outgoing = jnp.dot(place, scaled, preferred_element_type=jnp.float32).astype(jnp.bfloat16)
    outgoing = outgoing.reshape(expert_count, capacity, seq.shape[1])
    arrived = lax.all_to_all(outgoing, "node", split_axis=0, concat_axis=0, tiled=True)
    flat_rows = arrived.reshape(-1, seq.shape[1])
    gate_shard = w_gate[0]
    up_shard = w_up[0]
    down_shard = w_down[0]
    piece = lax.all_gather(flat_rows, "local", axis=0, tiled=True)
    gate = jnp.dot(piece, gate_shard, preferred_element_type=jnp.float32)
    upper = jnp.dot(piece, up_shard, preferred_element_type=jnp.float32)
    hidden = (jax.nn.silu(gate) * upper).astype(jnp.bfloat16)
    picked = hidden
    result = lax.psum_scatter(
        jnp.dot(picked, down_shard, preferred_element_type=jnp.float32).astype(jnp.bfloat16),
        "local",
        scatter_dimension=0,
        tiled=True,
    )
    return result[None]


def solution(mesh):
    in_specs = (
        P("node", None),
        P(),
        P(None, "local"),
        P("local", None),
        P("local", None),
        P(("node", "local"), None),
        P(),
        P(("node", "local"), None),
        P("node", None, "local"),
        P("node", None, "local"),
        P("node", "local", None),
    )
    out_specs = P("node", "local", None)
    return jax.shard_map(
        on_device, mesh=mesh, in_specs=in_specs, out_specs=out_specs, check_vma=False
    )
```

profile of v0, /device:TPU:1, one launch (start us, length us, event | category | flops | bytes accessed | tf_op | source)
XLA Modules:
  0.0 502.0 jit_solution(7583077141259206168)
XLA Ops:
  6.5 1.3 copy.14
  7.9 0.2 convert_reduce_fusion
  8.1 0.2 multiply_reduce_fusion
  8.3 3.6 convolution_convert_fusion.3
  11.9 0.0 all-reduce.6.cloned.1.call-start
  12.0 0.9 convert_element_type.45
  12.9 85.2 %all-reduce.4.cloned.1.call-done = bf16[128,1408]{0,1:T(8,128)(2,1)} async-done(((bf16[128,1408]{0,1:T(8,128)(2,1)}), bf16[128,1408]{0,1:T(8,128)(2,1)}) %all-reduce.4.cloned.1.call-update) | async-done | bytes 360464 | tf_op jit(solution)/shard_map/psum | solution.py:34
  98.1 2.8 convolution_convert_fusion.1
  100.9 0.0 all-gather.2.cloned.1.call-start
  101.0 0.1 copy.12
  101.1 0.2 reduce_window_sum.11
  101.3 0.6 dynamic-slice
  102.6 85.1 %all-reduce.6.cloned.1.call-done = bf16[128,5120]{1,0:T(8,128)(2,1)} async-done(((bf16[128,5120]{1,0:T(8,128)(2,1)}), bf16[128,5120]{1,0:T(8,128)(2,1)}) %all-reduce.6.cloned.1.call-update) | async-done | bytes 1310736
  187.7 1.0 constant_dynamic-slice_fusion
  188.7 1.7 fusion.8
  190.4 1.6 convolution_convert_fusion.2
  192.0 2.3 reshape.36
  194.3 24.5 %all_to_all.5 = bf16[8,14,5120]{2,1,0:T(8,128)(2,1)} all-to-all(bf16[8,14,5120]{2,1,0:T(8,128)(2,1)} %reshape.36), channel_id=1, replica_groups=mesh['node'=8,'local'=16] {'node'}, dimensions={0} | all-to-all | bytes 2293760 | tf_op jit(solution)/shard_map/all_to_all | solution.py:63
  218.8 2.3 reshape.37
  221.1 0.2 reduce-scatter.2.cloned.1.call-start
  221.3 116.9 %all-gather.2.cloned.1.call-done = bf16[1792,5120]{1,0:T(8,128)(2,1)} async-done(((bf16[112,5120]{1,0:T(8,128)(2,1)}), bf16[1792,5120]{1,0:T(8,128)(2,1)}) %all-gather.2.cloned.1.call-update) | async-done | bytes 18350096 | tf_op jit(solution)/shard_map/all_gather | solution.py:68
  338.2 13.4 %fusion.2 = f32[1792,256]{1,0:T(8,128)} fusion(bf16[1792,5120]{1,0:T(8,128)(2,1)} %all-gather.2.cloned.1.call-done, bf16[1,5120,256]{2,1,0:T(8,128)(2,1)} %param.19), kind=kOutput, calls=%fused_computation.6 | convolution fusion | flops 4697620480 | bytes 22806528 | tf_op jit(solution)/shard_map/dot_general | solution.py:69
  351.6 25.7 %convolution_convert_fusion = bf16[1792,5120]{1,0:T(8,128)(2,1)} fusion(bf16[1,256,5120]{2,1,0:T(8,128)(2,1)S(1)} %copy-done, bf16[1792,5120]{1,0:T(8,128)(2,1)} %all-gather.2.cloned.1.call-done, bf16[1,5120,256]{2,1,0:T(8,128)(2,1)} %param.20, f32[1792,256]{1,0:T(8,128)} %fusion.2), kind=kOutput, calls=%fused_computation | convolution fusion | flops 9407168512 | bytes 43778048 | tf_op jit(solution)/shard_map/dot_general | solution.py:74
  377.4 118.1 %reduce-scatter.2.cloned.1.call-done = bf16[112,5120]{1,0:T(8,128)(2,1)} async-done(((bf16[1792,5120]{1,0:T(8,128)(2,1)}), bf16[112,5120]{1,0:T(8,128)(2,1)}) %reduce-scatter.2.cloned.1.call-update) | async-done | bytes 1146896 | tf_op jit(solution)/shard_map/reduce_scatter | solution.py:73
  (23 shorter events, 0.2 us)
Async XLA Ops:
  6.5 345.1 %copy-start = (bf16[1,256,5120]{2,1,0:T(8,128)(2,1)S(1)}, bf16[1,256,5120]{2,1,0:T(8,128)(2,1)}, u32[]{:S(2)}) copy-start(bf16[1,256,5120]{2,1,0:T(8,128)(2,1)} %param.21) | copy-start | bytes 7864324
  6.5 91.5 %all-reduce.4.cloned.1.call-start = ((), (), s32[]{:S(2)}) async-start(), calls=%async_computation.2 | async-start | bytes 720896 | tf_op jit(solution)/shard_map/psum | solution.py:34
  11.9 175.8 %all-reduce.6.cloned.1.call-start = ((), (), s32[]{:S(2)}) async-start(), calls=%async_computation.5 | async-start | bytes 2621440
  12.0 89.0 %copy-start.1 = (s32[128,1]{0,1:T(1,128)S(1)}, s32[128,1]{0,1:T(1,128)}, u32[]{:S(2)}) copy-start(s32[128,1]{0,1:T(1,128)} %param.18) | copy-start | bytes 1540
  12.0 89.3 %copy-start.4 = (u32[128]{0:T(128)S(1)}, u32[128]{0:T(128)}, u32[]{:S(2)}) copy-start(u32[128]{0:T(128)} %constant.45) | copy-start | bytes 1540
  12.9 175.8 %copy-start.3 = (bf16[5120,8]{0,1:T(8,128)(2,1)S(1)}, bf16[5120,8]{0,1:T(8,128)(2,1)}, u32[]{:S(2)}) copy-start(bf16[5120,8]{0,1:T(8,128)(2,1)} %param.17) | copy-start | bytes 245764
  100.9 237.3 %all-gather.2.cloned.1.call-start = ((), (), s32[]{:S(2)}) async-start(), calls=%async_computation.3 | async-start | bytes 19496960 | tf_op jit(solution)/shard_map/all_gather | solution.py:68
  187.7 2.8 copy-start.2
  221.1 274.4 %reduce-scatter.2.cloned.1.call-start = ((), (), s32[]{:S(2)}) async-start(), calls=%async_computation.4 | async-start | bytes 19496960 | tf_op jit(solution)/shard_map/reduce_scatter | solution.py:73
Sparse Core Ops, SparseCore 0:
  12.0 85.9 all-reduce.3
  101.3 86.2 all-reduce.5
  221.2 116.9 all-gather.1
  377.5 117.9 reduce-scatter.1
where the time goes:
time: 502 us
  waiting for transfers between devices  405 us (81%)
  matrix products  48.8 us (10%)
  blocking collectives  24.5 us (5%)
  between operations  13.9 us (3%)
  local copies, waits for them, and re-layouts  7.69 us (2%)
    reduce_scatter x1, waiting for transfers between devices, on_device(): lax.psum_scatter(jnp.dot(picked, down_shard, preferred_element_type=jnp.f...  118 us
    all_gather x1, waiting for transfers between devices, on_device(): piece = lax.all_gather(flat_rows, 'local', axis=0, tiled=True)  117 us
    psum x1, waiting for transfers between devices, on_device(): lax.psum(partial_sum.astype(jnp.bfloat16), 'local').astype(jnp.float32)  85.2 us
    unnamed x5, waiting for transfers between devices  85.1 us
    dot_general x1, matrix products, on_device(): jnp.dot(picked, down_shard, preferred_element_type=jnp.float32)  25.7 us
    all_to_all x1, blocking collectives, on_device(): lax.all_to_all(outgoing, 'node', split_axis=0, concat_axis=0, tiled=True)  24.5 us
    dot_general x1, matrix products, on_device(): gate = jnp.dot(piece, gate_shard, preferred_element_type=jnp.float32)  13.4 us
  transfers between devices with their start and end apart: 4, of which 4 were waited for; matrix products, arithmetic and copies ran while one was open for 0% of the time, Pallas kernels for 0%

commit v1 on v0

v1 whole, which is shorter than its diff:
```python
import jax
import jax.numpy as jnp
from jax import lax
from jax.experimental import pallas as pl
from jax.experimental.pallas import tpu as pltpu
from jax.sharding import PartitionSpec as P

MESH = pl.DeviceIdType.MESH
BF = jnp.bfloat16
F32 = jnp.float32
SIDE = 4
PAD = 16


def remote(src, dst, send_sem, recv_sem, device):
    return pltpu.make_async_remote_copy(
        src_ref=src,
        dst_ref=dst,
        send_sem=send_sem,
        recv_sem=recv_sem,
        device_id=device,
        device_id_type=MESH,
    )


def greet(devices):
    barrier = pltpu.get_barrier_semaphore()
    for device in devices:
        pl.semaphore_signal(barrier, inc=1, device_id=device, device_id_type=MESH)
    pl.semaphore_wait(barrier, len(devices))


def vision_kernel(
    n_local,
    capacity,
    patches_ref,
    gain_ref,
    up_ref,
    down_ref,
    adapter_ref,
    text_ref,
    router_ref,
    ids_ref,
    out_ref,
    part_send,
    part_recv,
    patch_blocks,
    embed_send,
    embed_recv,
    sems,
):
    node, local = lax.axis_index("node"), lax.axis_index("local")
    peers = [(node, lax.rem(local + k, n_local)) for k in range(1, n_local)]
    greet(peers)

    rows, width = patches_ref.shape
    block = width // n_local
    values = patches_ref[...].astype(F32)
    center = jnp.mean(values, axis=-1, keepdims=True)
    spread = jnp.mean((values - center) ** 2, axis=-1, keepdims=True)
    normed = ((values - center) * lax.rsqrt(spread + 1e-05) * gain_ref[...]).astype(BF)
    inner = jax.nn.gelu(
        jnp.dot(normed, up_ref[...], preferred_element_type=F32), approximate=True
    ).astype(BF)
    partial_sum = jnp.dot(inner, down_ref[...], preferred_element_type=F32)
    for index in range(n_local):
        low = index * block
        part_send[index, :, 0:block] = partial_sum[:, low : low + block].astype(BF)
        patch_blocks[index, :, 0:block] = values[:, low : low + block].astype(BF)

    first = []
    for k in range(1, n_local):
        copy = remote(
            part_send.at[peers[k - 1][1]],
            part_recv.at[k],
            sems.at[0, k],
            sems.at[1, k],
            peers[k - 1],
        )
        copy.start()
        first.append(copy)

    text_rows, model = text_ref.shape
    all_rows = ids_ref.shape[0]
    experts = router_ref.shape[1]
    chosen = ids_ref[...]
    table = (
        chosen == lax.broadcasted_iota(jnp.int32, (all_rows, experts), 1)
    ).astype(F32)
    earlier = (
        lax.broadcasted_iota(jnp.int32, (all_rows, all_rows), 0)
        > lax.broadcasted_iota(jnp.int32, (all_rows, all_rows), 1)
    ).astype(BF)
    counts = jnp.dot(earlier, table.astype(BF), preferred_element_type=F32)
    rank = jnp.sum(counts * table, axis=1, keepdims=True).astype(jnp.int32)
    slot = jnp.where(rank < capacity, chosen * PAD + rank, -1)
    place = jnp.transpose(
        (slot == lax.broadcasted_iota(jnp.int32, (all_rows, experts * PAD), 1)).astype(F32)
    ).astype(BF)
    logits = jnp.dot(text_ref[...], router_ref[...], preferred_element_type=F32)
    score = jax.nn.sigmoid(
        jnp.sum(logits * table[0:text_rows], axis=1, keepdims=True)
    )
    step = 512

    def place_text(index, carry):
        columns = pl.ds(pl.multiple_of(index * step, step), step)
        scaled = text_ref[:, columns].astype(F32) * score
        scaled = jnp.concatenate(
            [scaled, jnp.zeros((all_rows - text_rows, step), F32)], axis=0
        ).astype(BF)
        sent = jnp.dot(place, scaled, preferred_element_type=F32).astype(BF)
        for expert in range(experts):
            out_ref[expert, :, columns] = sent[expert * PAD : (expert + 1) * PAD]
        return carry

    lax.fori_loop(0, model // step, place_text, 0)

    total = part_send[local, :, 0:block].astype(F32)
    for k in range(1, n_local):
        first[k - 1].wait_recv()
        total = total + part_recv[k, :, 0:block].astype(F32)
    vision = (patch_blocks[local, :, 0:block].astype(F32) + total).astype(BF)

    half = model // 2
    own = rows // n_local
    wide = 640

    def embed_part(index, carry):
        low = pl.ds(pl.multiple_of(index * wide, 128), wide)
        high = pl.ds(pl.multiple_of(index * wide + half, 128), wide)
        left = jnp.dot(vision, adapter_ref[:, low], preferred_element_type=F32)
        right = jnp.dot(vision, adapter_ref[:, high], preferred_element_type=F32)
        for j in range(n_local):
            embed_send[j, :, low] = jnp.concatenate(
                [left[j * own : (j + 1) * own], right[j * own : (j + 1) * own]], axis=0
            ).astype(BF)
        return carry

    lax.fori_loop(0, half // wide, embed_part, 0)

    second = []
    for k in range(1, n_local):
        copy = remote(
            embed_send.at[peers[k - 1][1]],
            embed_recv.at[k],
            sems.at[2, k],
            sems.at[3, k],
            peers[k - 1],
        )
        copy.start()
        second.append(copy)
    for k in range(1, n_local):
        second[k - 1].wait_recv()

    embed = embed_send[local].astype(F32)
    for k in range(1, n_local):
        embed = embed + embed_recv[k].astype(F32)
    embed = embed.astype(BF).astype(F32)
    image = jnp.dot(
        embed[0:own].astype(BF), router_ref[0:half, :], preferred_element_type=F32
    ) + jnp.dot(
        embed[own : 2 * own].astype(BF), router_ref[half:model, :], preferred_element_type=F32
    )
    image_score = jax.nn.sigmoid(
        jnp.sum(image * table[text_rows:all_rows], axis=1, keepdims=True)
    )
    for part in range(2):
        for low in range(0, half, step):
            columns = slice(part * half + low, part * half + low + step)
            scaled = embed[part * own : (part + 1) * own, low : low + step] * image_score
            scaled = jnp.concatenate(
                [jnp.zeros((text_rows, step), F32), scaled], axis=0
            ).astype(BF)
            sent = jnp.dot(place, scaled, preferred_element_type=F32)
            for expert in range(experts):
                out_ref[expert, :, columns] = (
                    out_ref[expert, :, columns].astype(F32)
                    + sent[expert * PAD : (expert + 1) * PAD]
                ).astype(BF)
    for copy in first + second:
        copy.wait_send()


def expert_kernel(
    n_node,
    capacity,
    slots_ref,
    gate_hbm,
    up_hbm,
    down_hbm,
    out_ref,
    gate_ref,
    up_ref,
    down_ref,
    arrived,
    held,
    hidden,
    halves,
    fulls,
    load_sem,
    node_sem,
    gather_sem,
    reduce_sem,
):
    node, local = lax.axis_index("node"), lax.axis_index("local")
    core = lax.rem(node, 2)
    x, y = local // SIDE, lax.rem(local, SIDE)
    p1, p2 = jnp.where(core == 0, x, y), jnp.where(core == 0, y, x)
    s1, s2 = jnp.where(core == 0, SIDE, 1), jnp.where(core == 0, 1, SIDE)

    def shift(p, d):
        return lax.rem(p + d + SIDE, SIDE)

    def device(d1, d2):
        return (node, shift(p1, d1) * s1 + shift(p2, d2) * s2)

    def blk(d1, d2):
        return shift(p1, d1) * SIDE + shift(p2, d2)

    peers = [(lax.rem(node + k, n_node), local) for k in range(1, n_node)]
    rings = [(device(1, 0), device(-1, 0)), (device(0, 1), device(0, -1))]
    greet(peers + list(rings[0]) + list(rings[1]))

    loads = [
        pltpu.make_async_copy(gate_hbm.at[0], gate_ref, load_sem.at[0]),
        pltpu.make_async_copy(up_hbm.at[0], up_ref, load_sem.at[1]),
        pltpu.make_async_copy(down_hbm.at[0], down_ref, load_sem.at[2]),
    ]
    sends = []
    for k in range(1, n_node):
        copy = remote(
            slots_ref.at[peers[k - 1][0]],
            arrived.at[node],
            node_sem.at[0, k],
            node_sem.at[1, k],
            peers[k - 1],
        )
        copy.start()
        sends.append(copy)
    for load in loads:
        load.start()
    mine = pltpu.make_async_copy(slots_ref.at[node], arrived.at[node], load_sem.at[3])
    mine.start()
    for k in range(1, n_node):
        source = lax.rem(node + n_node - k, n_node)
        remote(
            arrived.at[source],
            arrived.at[source],
            node_sem.at[0, k],
            node_sem.at[1, k],
            peers[k - 1],
        ).wait_recv()
    mine.wait()

    rows, model = held.shape[1], held.shape[2]
    half = model // 2
    step = 512
    target = lax.broadcasted_iota(jnp.int32, (rows, n_node * PAD), 0)
    origin = lax.broadcasted_iota(jnp.int32, (rows, n_node * PAD), 1)
    pick = (target // capacity * PAD + lax.rem(target, capacity) == origin).astype(BF)
    home = blk(0, 0)

    def compact(index, carry):
        columns = pl.ds(pl.multiple_of(index * step, step), step)
        held[home, :, columns] = jnp.dot(
            pick,
            arrived[:, :, columns].reshape(n_node * PAD, step),
            preferred_element_type=F32,
        ).astype(BF)
        return carry

    lax.fori_loop(0, model // step, compact, 0)

    depth = 1280

    def ffn_in(block):
        def body(index, carry):
            gate, upper = carry
            deep = pl.ds(pl.multiple_of(index * depth, depth), depth)
            piece = held[block, :, deep]
            return (
                gate + jnp.dot(piece, gate_ref[deep, :], preferred_element_type=F32),
                upper + jnp.dot(piece, up_ref[deep, :], preferred_element_type=F32),
            )

        zero = jnp.zeros((rows, gate_ref.shape[1]), F32)
        gate, upper = lax.fori_loop(0, model // depth, body, (zero, zero))
        hidden[block] = (jax.nn.silu(gate) * upper).astype(BF)

    gather_waits = []

    def ring_send(op, ring, block, way):
        copy = remote(
            held.at[block],
            held.at[block],
            gather_sem.at[0, op, way],
            gather_sem.at[1, op, way],
            rings[ring][way],
        )
        copy.start()
        gather_waits.append(copy)

    def ring_recv(op, ring, block, way):
        remote(
            held.at[block],
            held.at[block],
            gather_sem.at[0, op, way],
            gather_sem.at[1, op, way],
            rings[ring][way],
        ).wait_recv()

    def half_copy(op, ring, block, way):
        part = held.at[block, :, pl.ds(way * half, half)]
        return remote(
            part,
            part,
            gather_sem.at[0, op, 2 + way],
            gather_sem.at[1, op, 2 + way],
            rings[ring][way],
        )

    def half_send(op, ring, block, way):
        copy = half_copy(op, ring, block, way)
        copy.start()
        gather_waits.append(copy)

    def half_recv(op, ring, block, way):
        half_copy(op, ring, block, way).wait_recv()

    for way in range(2):
        ring_send(0, 0, blk(0, 0), way)
    for way in range(2):
        ring_send(1, 1, blk(0, 0), way)
    loads[0].wait()
    loads[1].wait()
    ffn_in(blk(0, 0))
    sides = (-1, 1)
    for way in range(2):
        block = blk(sides[way], 0)
        ring_recv(0, 0, block, way)
        half_send(0, 0, block, way)
        for out in range(2):
            ring_send(2 + way, 1, block, out)
    for way in range(2):
        ffn_in(blk(sides[way], 0))
    for way in range(2):
        block = blk(0, sides[way])
        ring_recv(1, 1, block, way)
        half_send(1, 1, block, way)
    for way in range(2):
        half_recv(0, 0, blk(2, 0), way)
    for way in range(2):
        ring_send(4, 1, blk(2, 0), way)
    for way in range(2):
        ffn_in(blk(0, sides[way]))
    ffn_in(blk(2, 0))
    for way in range(2):
        half_recv(1, 1, blk(0, 2), way)
    ffn_in(blk(0, 2))
    for op, d1 in ((2, -1), (3, 1), (4, 2)):
        for way in range(2):
            block = blk(d1, sides[way])
            ring_recv(op, 1, block, way)
            half_send(op, 1, block, way)
        for way in range(2):
            ffn_in(blk(d1, sides[way]))
        if op > 2:
            before = {3: -1, 4: 1}[op]
            for way in range(2):
                half_recv(op - 1, 1, blk(before, 2), way)
            ffn_in(blk(before, 2))
    for way in range(2):
        half_recv(4, 1, blk(2, 2), way)
    ffn_in(blk(2, 2))
    loads[2].wait()

    reduce_waits = []
    order = (2, 1, -1, 0)

    def part_copy(op, ring, block, way):
        return remote(
            held.at[block, :, pl.ds(way * half, half)],
            halves.at[op, way],
            reduce_sem.at[0, op, way],
            reduce_sem.at[1, op, way],
            rings[ring][way],
        )

    def full_copy(op, ring, block, way):
        return remote(
            held.at[block],
            fulls.at[op, way],
            reduce_sem.at[0, op, 2 + way],
            reduce_sem.at[1, op, 2 + way],
            rings[ring][way],
        )

    def start(copy):
        copy.start()
        reduce_waits.append(copy)

    def ffn_out(block, dest, terms):
        for part in range(2):

            def body(index, carry):
                low = pl.multiple_of(index * step, step)
                columns = pl.ds(pl.multiple_of(low + part * half, step), step)
                value = jnp.dot(
                    hidden[block], down_ref[:, columns], preferred_element_type=F32
                )
                for term in terms:
                    if term[0] == "full":
                        value = value + fulls[term[1], term[2], :, columns].astype(F32)
                    elif term[2] == part:
                        value = value + halves[term[1], term[2], :, pl.ds(low, step)].astype(F32)
                dest[:, columns] = value.astype(BF)
                return carry

            lax.fori_loop(0, half // step, body, 0)

    def far(k):
        block = blk(order[k], 2)
        ffn_out(block, held.at[block], ())
        for way in range(2):
            start(part_copy(k, 1, block, way))

    def near(k):
        for way in range(2):
            block = blk(order[k], (1, -1)[way])
            part_copy(k, 1, block, way).wait_recv()
            ffn_out(block, held.at[block], (("half", k, way),))
            start(full_copy(k, 1, block, way))

    def own(k):
        block = blk(order[k], 0)
        for way in range(2):
            full_copy(k, 1, block, way).wait_recv()
        terms = [("full", k, 0), ("full", k, 1)]
        dest = held.at[block]
        if k in (1, 2):
            part_copy(4, 0, block, k - 1).wait_recv()
            terms.append(("half", 4, k - 1))
        if k == 3:
            for way in range(2):
                full_copy(4, 0, block, way).wait_recv()
                terms.append(("full", 4, way))
            dest = out_ref
        ffn_out(block, dest, terms)
        if k == 0:
            for way in range(2):
                start(part_copy(4, 0, block, way))
        elif k in (1, 2):
            start(full_copy(4, 0, block, k - 1))

    for k in range(4):
        far(k)
    for copy in gather_waits:
        copy.wait_send()
    near(0)
    near(1)
    own(0)
    near(2)
    own(1)
    near(3)
    own(2)
    own(3)
    for copy in sends + reduce_waits:
        copy.wait_send()


def on_device(n_node, n_local):
    def run(
        patches,
        norm_gain,
        vit_up,
        vit_down,
        adapter,
        text_rows,
        router,
        expert_ids,
        w_gate,
        w_up,
        w_down,
    ):
        vmem = pl.BlockSpec(memory_space=pltpu.VMEM)
        hbm = pl.BlockSpec(memory_space=pl.ANY)
        row_count, model = expert_ids.shape[0], adapter.shape[1]
        experts = router.shape[1]
        capacity = 7 * row_count // (8 * n_node)
        rows, width = patches.shape
        lanes = 128 * ((width // n_local + 127) // 128)
        slots = pl.pallas_call(
            lambda *refs: vision_kernel(n_local, capacity, *refs),
            out_shape=jax.ShapeDtypeStruct((experts, PAD, model), BF),
            in_specs=[vmem] * 8,
            out_specs=vmem,
            scratch_shapes=[
                pltpu.VMEM((n_local, rows, lanes), BF),
                pltpu.VMEM((n_local, rows, lanes), BF),
                pltpu.VMEM((n_local, rows, lanes), BF),
                pltpu.VMEM((n_local, 2 * rows // n_local, model // 2), BF),
                pltpu.VMEM((n_local, 2 * rows // n_local, model // 2), BF),
                pltpu.SemaphoreType.DMA((4, n_local)),
            ],
            compiler_params=pltpu.CompilerParams(
                collective_id=0,
                has_side_effects=True,
                vmem_limit_bytes=48 * 2**20,
            ),
        )(
            patches,
            norm_gain.reshape(1, -1),
            vit_up,
            vit_down,
            adapter,
            text_rows,
            router,
            expert_ids,
        )
        own_rows = n_node * capacity
        units = w_gate.shape[2]
        result = pl.pallas_call(
            lambda *refs: expert_kernel(n_node, capacity, *refs),
            out_shape=jax.ShapeDtypeStruct((own_rows, model), BF),
            in_specs=[vmem, hbm, hbm, hbm],
            out_specs=vmem,
            scratch_shapes=[
                pltpu.VMEM((model, units), BF),
                pltpu.VMEM((model, units), BF),
                pltpu.VMEM((units, model), BF),
                pltpu.VMEM((n_node, PAD, model), BF),
                pltpu.VMEM((n_local, own_rows, model), BF),
                pltpu.VMEM((n_local, own_rows, units), BF),
                pltpu.VMEM((5, 2, own_rows, model // 2), BF),
                pltpu.VMEM((5, 2, own_rows, model), BF),
                pltpu.SemaphoreType.DMA((4,)),
                pltpu.SemaphoreType.DMA((2, n_node)),
                pltpu.SemaphoreType.DMA((2, 5, 4)),
                pltpu.SemaphoreType.DMA((2, 5, 4)),
            ],
            compiler_params=pltpu.CompilerParams(
                collective_id=1,
                has_side_effects=True,
                vmem_limit_bytes=58 * 2**20,
            ),
        )(slots, w_gate, w_up, w_down)
        return result[None]

    return run


def solution(mesh):
    in_specs = (
        P("node", None),
        P(),
        P(None, "local"),
        P("local", None),
        P("local", None),
        P(("node", "local"), None),
        P(),
        P(("node", "local"), None),
        P("node", None, "local"),
        P("node", None, "local"),
        P("node", "local", None),
    )
    out_specs = P("node", "local", None)
    return jax.shard_map(
        on_device(mesh.shape["node"], mesh.shape["local"]),
        mesh=mesh,
        in_specs=in_specs,
        out_specs=out_specs,
        check_vma=False,
    )
```

time: 502 us -> 271 us (0.54)
  waiting for transfers between devices: 405 us -> 0 us
  Pallas kernels: 0 us -> 257 us
  matrix products: 48.8 us -> 0 us
  blocking collectives: 24.5 us -> 0 us
  between operations: 13.9 us -> 0.06 us
    pallas_call x0 -> x2, Pallas kernels: none -> 257 us  [the longest x1 226 us: run(): pl.pallas_call(lambda *refs: expert_kernel(n_node, capacity, *refs), out_...]
    reduce_scatter x1 -> x0, waiting for transfers between devices: 118 us -> none  [on_device(): lax.psum_scatter(jnp.dot(picked, down_shard, preferred_element_type=jnp.f...]
    all_gather x1 -> x0, waiting for transfers between devices: 117 us -> none  [on_device(): piece = lax.all_gather(flat_rows, 'local', axis=0, tiled=True)]
    psum x1 -> x0, waiting for transfers between devices: 85.2 us -> none  [on_device(): lax.psum(partial_sum.astype(jnp.bfloat16), 'local').astype(jnp.float32)]
    unnamed x5 -> x0, waiting for transfers between devices: 85.1 us -> none
    dot_general x6 -> x0, matrix products: 48.8 us -> none  [the longest x1 25.7 us: on_device(): jnp.dot(picked, down_shard, preferred_element_type=jnp.float32)]
    all_to_all x1 -> x0, blocking collectives: 24.5 us -> none  [on_device(): lax.all_to_all(outgoing, 'node', split_axis=0, concat_axis=0, tiled=True)]
    unnamed x13 -> x16, local copies, waits for them, and re-layouts: 2.97 us -> 10.1 us
  transfers between devices with their start and end apart: 4 -> 0, of which waited for: 4 -> 0; matrix products, arithmetic and copies ran while one was open for 0% -> 0% of each run, Pallas kernels for 0% -> 0%
where the time goes in v1:
time: 271 us; the launch traced here: 268 us
  Pallas kernels  257 us (95%)
  local copies, waits for them, and re-layouts  10.9 us (4%)
    pallas_call x1, Pallas kernels, run(): pl.pallas_call(lambda *refs: expert_kernel(n_node, capacity, *refs), out_...  226 us
    pallas_call x1, Pallas kernels, run(): pl.pallas_call(lambda *refs: vision_kernel(n_local, capacity, *refs), out...  31 us
    unnamed x16, local copies, waits for them, and re-layouts  10.1 us

profile of v1, /device:TPU:1, one launch (start us, length us, event | category | flops | bytes accessed | tf_op | source)
XLA Modules:
  0.0 268.4 jit_solution(5089681244470353561)
XLA Ops:
  0.0 0.0 copy-start.5
  0.0 0.7 reshape.3.refs_1_
  0.7 0.8 copy.14.refs_7_
  1.5 0.0 copy-start.1
  1.5 0.0 copy-start.2
  1.5 2.3 copy.12.refs_2_
  3.8 0.0 copy-done.5
  3.9 1.5 copy.13.refs_6_
  5.3 0.0 copy-done.1
  5.3 0.0 copy-done.2
  5.3 0.0 copy-start.3
  5.3 1.2 copy-done.3
  6.5 0.0 copy-start.4
  6.5 1.0 copy-done.4
  7.5 31.0 %shard_map.109.refs_0_ = bf16[8,16,5120]{2,1,0:T(8,128)(2,1)S(1)} custom-call(bf16[128,1408]{1,0:T(8,128)(2,1)S(1)} %copy-done.4, f32[1,1408]{1,0:T(1,128)S(1)} %reshape.3.refs_1_, bf16[1408,352]{1,0:T(8,128)(2,1)S(1)} %copy.12.refs_2_, bf16[352,1408]{1,0:T(8,128)(2,1)S(1)} %copy-done.2, bf16[88,5120]{1,0:T(8,128)(2,1)S(1)} %copy-done.3, ...), custom_call_target="tpu_custom_call" | custom-call | tf_op jit(solution)/shard_map/pallas_call | solution.py:493
  38.6 0.0 copy-start
  38.6 1.1 copy-done
  39.6 226.4 %shard_map.110 = bf16[112,5120]{1,0:T(8,128)(2,1)} custom-call(bf16[8,16,5120]{2,1,0:T(8,128)(2,1)} %copy-done, bf16[1,5120,256]{2,1,0:T(8,128)(2,1)} %refs_1_.1, bf16[1,5120,256]{2,1,0:T(8,128)(2,1)} %refs_2_.2, bf16[1,256,5120]{2,1,0:T(8,128)(2,1)} %refs_3_.3), custom_call_target="tpu_custom_call" | custom-call | tf_op jit(solution)/shard_map/pallas_call | solution.py:523
  266.0 2.3 copy.16
Async XLA Ops:
  0.0 3.8 %copy-start.5 = (bf16[5120,8]{0,1:T(8,128)(2,1)S(1)}, bf16[5120,8]{0,1:T(8,128)(2,1)}, u32[]{:S(2)}) copy-start(bf16[5120,8]{0,1:T(8,128)(2,1)} %param.17) | copy-start | bytes 245764
  1.5 3.8 %copy-start.1 = (bf16[120,5120]{1,0:T(8,128)(2,1)S(1)}, bf16[120,5120]{1,0:T(8,128)(2,1)}, u32[]{:S(2)}) copy-start(bf16[120,5120]{1,0:T(8,128)(2,1)} %refs_5_.1) | copy-start | bytes 3686404
  1.5 3.8 %copy-start.2 = (bf16[352,1408]{1,0:T(8,128)(2,1)S(1)}, bf16[352,1408]{1,0:T(8,128)(2,1)}, u32[]{:S(2)}) copy-start(bf16[352,1408]{1,0:T(8,128)(2,1)} %refs_3_.2) | copy-start | bytes 2973700
  5.3 1.2 copy-start.3
  6.5 1.0 copy-start.4
  38.6 1.1 copy-start

commit v2 on v1

v2 whole, which is shorter than its diff:
```python
import functools

import jax
import jax.numpy as jnp
from jax import lax
from jax.experimental import pallas as pl
from jax.experimental.pallas import tpu as pltpu
from jax.sharding import PartitionSpec as P

MESH = pl.DeviceIdType.MESH
BF = jnp.bfloat16
F32 = jnp.float32
SIDE = 4
PAD = 16


def remote(src, dst, send_sem, recv_sem, device):
    return pltpu.make_async_remote_copy(
        src_ref=src,
        dst_ref=dst,
        send_sem=send_sem,
        recv_sem=recv_sem,
        device_id=device,
        device_id_type=MESH,
    )


def greet(devices):
    barrier = pltpu.get_barrier_semaphore()
    for device in devices:
        pl.semaphore_signal(barrier, inc=1, device_id=device, device_id_type=MESH)
    pl.semaphore_wait(barrier, len(devices))


def vision_kernel(
    n_node,
    n_local,
    capacity,
    patches_ref,
    gain_ref,
    up_ref,
    down_ref,
    adapter_ref,
    text_ref,
    router_ref,
    ids_ref,
    gate_hbm,
    up_hbm,
    down_hbm,
    out_ref,
    gate_swap,
    up_swap,
    down_swap,
    slots,
    arrived,
    part_send,
    part_recv,
    patch_blocks,
    embed_send,
    embed_recv,
    sems,
    node_sem,
    swap_sem,
):
    node, local = lax.axis_index("node"), lax.axis_index("local")
    peers = [(node, lax.rem(local + k, n_local)) for k in range(1, n_local)]
    core = lax.rem(node, 2)
    x, y = local // SIDE, lax.rem(local, SIDE)
    column = [(lax.rem(node + k, n_node), local) for k in range(1, n_node)]
    sibling = node + 1 - 2 * core
    beside = [(sibling, lax.rem(x + d, SIDE) * SIDE + y) for d in (SIDE - 1, 1)]
    greet(peers + column + beside)

    units = gate_hbm.shape[2]
    swaps = []
    for way in range(2):
        part = pl.ds(way * (units // 2), units // 2)
        for index, (here, there) in enumerate(
            (
                (gate_hbm.at[0, :, part], gate_swap.at[:, part]),
                (up_hbm.at[0, :, part], up_swap.at[:, part]),
                (down_hbm.at[0, part, :], down_swap.at[part, :]),
            )
        ):
            swaps.append(
                remote(
                    here,
                    there,
                    swap_sem.at[0, way, index],
                    swap_sem.at[1, way, index],
                    beside[way],
                )
            )

    @pl.when(core != lax.rem(x, 2))
    def _():
        for copy in swaps:
            copy.start()

    rows, width = patches_ref.shape
    block = width // n_local
    values = patches_ref[...].astype(F32)
    center = jnp.mean(values, axis=-1, keepdims=True)
    spread = jnp.mean((values - center) ** 2, axis=-1, keepdims=True)
    normed = ((values - center) * lax.rsqrt(spread + 1e-05) * gain_ref[...]).astype(BF)
    inner = jax.nn.gelu(
        jnp.dot(normed, up_ref[...], preferred_element_type=F32), approximate=True
    ).astype(BF)
    partial_sum = jnp.dot(inner, down_ref[...], preferred_element_type=F32)
    for index in range(n_local):
        low = index * block
        part_send[index, :, 0:block] = partial_sum[:, low : low + block].astype(BF)
        patch_blocks[index, :, 0:block] = values[:, low : low + block].astype(BF)

    first = []
    for k in range(1, n_local):
        copy = remote(
            part_send.at[peers[k - 1][1]],
            part_recv.at[k],
            sems.at[0, k],
            sems.at[1, k],
            peers[k - 1],
        )
        copy.start()
        first.append(copy)

    text_rows, model = text_ref.shape
    all_rows = ids_ref.shape[0]
    experts = router_ref.shape[1]
    chosen = ids_ref[...]
    table = (
        chosen == lax.broadcasted_iota(jnp.int32, (all_rows, experts), 1)
    ).astype(F32)
    earlier = (
        lax.broadcasted_iota(jnp.int32, (all_rows, all_rows), 0)
        > lax.broadcasted_iota(jnp.int32, (all_rows, all_rows), 1)
    ).astype(BF)
    counts = jnp.dot(earlier, table.astype(BF), preferred_element_type=F32)
    rank = jnp.sum(counts * table, axis=1, keepdims=True).astype(jnp.int32)
    slot = jnp.where(rank < capacity, chosen * PAD + rank, -1)
    place = jnp.transpose(
        (slot == lax.broadcasted_iota(jnp.int32, (all_rows, experts * PAD), 1)).astype(F32)
    ).astype(BF)
    logits = jnp.dot(text_ref[...], router_ref[...], preferred_element_type=F32)
    score = jax.nn.sigmoid(
        jnp.sum(logits * table[0:text_rows], axis=1, keepdims=True)
    )
    step = 512

    half = model // 2

    def place_text(part, index, carry):
        low = pl.multiple_of(index * step, step)
        columns = pl.ds(pl.multiple_of(part * half + low, step), step)
        scaled = text_ref[:, columns].astype(F32) * score
        scaled = jnp.concatenate(
            [scaled, jnp.zeros((all_rows - text_rows, step), F32)], axis=0
        ).astype(BF)
        sent = jnp.dot(place, scaled, preferred_element_type=F32).astype(BF)
        for expert in range(experts):
            slots[part, expert, :, pl.ds(low, step)] = sent[expert * PAD : (expert + 1) * PAD]
        return carry

    for part in range(2):
        lax.fori_loop(0, half // step, functools.partial(place_text, part), 0)

    total = part_send[local, :, 0:block].astype(F32)
    for k in range(1, n_local):
        first[k - 1].wait_recv()
        total = total + part_recv[k, :, 0:block].astype(F32)
    vision = (patch_blocks[local, :, 0:block].astype(F32) + total).astype(BF)

    own = rows // n_local
    wide = 640

    def embed_part(index, carry):
        low = pl.ds(pl.multiple_of(index * wide, 128), wide)
        high = pl.ds(pl.multiple_of(index * wide + half, 128), wide)
        left = jnp.dot(vision, adapter_ref[:, low], preferred_element_type=F32)
        right = jnp.dot(vision, adapter_ref[:, high], preferred_element_type=F32)
        for j in range(n_local):
            embed_send[j, :, low] = jnp.concatenate(
                [left[j * own : (j + 1) * own], right[j * own : (j + 1) * own]], axis=0
            ).astype(BF)
        return carry

    lax.fori_loop(0, half // wide, embed_part, 0)

    second = []
    for k in range(1, n_local):
        copy = remote(
            embed_send.at[peers[k - 1][1]],
            embed_recv.at[k],
            sems.at[2, k],
            sems.at[3, k],
            peers[k - 1],
        )
        copy.start()
        second.append(copy)
    for k in range(1, n_local):
        second[k - 1].wait_recv()

    embed = embed_send[local].astype(F32)
    for k in range(1, n_local):
        embed = embed + embed_recv[k].astype(F32)
    embed = embed.astype(BF).astype(F32)
    image = jnp.dot(
        embed[0:own].astype(BF), router_ref[0:half, :], preferred_element_type=F32
    ) + jnp.dot(
        embed[own : 2 * own].astype(BF), router_ref[half:model, :], preferred_element_type=F32
    )
    image_score = jax.nn.sigmoid(
        jnp.sum(image * table[text_rows:all_rows], axis=1, keepdims=True)
    )
    for part in range(2):
        for low in range(0, half, step):
            scaled = embed[part * own : (part + 1) * own, low : low + step] * image_score
            scaled = jnp.concatenate(
                [jnp.zeros((text_rows, step), F32), scaled], axis=0
            ).astype(BF)
            sent = jnp.dot(place, scaled, preferred_element_type=F32)
            for expert in range(experts):
                slots[part, expert, :, low : low + step] = (
                    slots[part, expert, :, low : low + step].astype(F32)
                    + sent[expert * PAD : (expert + 1) * PAD]
                ).astype(BF)

    third = []
    for k in range(1, n_node):
        target = column[k - 1][0]
        copy = remote(
            slots.at[lax.rem(target, 2), pl.ds(target // 2 * 2, 2)],
            arrived.at[node],
            node_sem.at[0, k],
            node_sem.at[1, k],
            column[k - 1],
        )
        copy.start()
        third.append(copy)
    mine = pltpu.make_async_copy(
        slots.at[core, pl.ds(node // 2 * 2, 2)], arrived.at[node], node_sem.at[0, 0]
    )
    mine.start()
    for k in range(1, n_node):
        source = arrived.at[lax.rem(node + n_node - k, n_node)]
        remote(source, source, node_sem.at[0, k], node_sem.at[1, k], column[k - 1]).wait_recv()
    mine.wait()

    kept = out_ref.shape[1]
    wanted = lax.broadcasted_iota(jnp.int32, (kept, n_node * PAD), 0)
    origin = lax.broadcasted_iota(jnp.int32, (kept, n_node * PAD), 1)
    pick = (wanted // capacity * PAD + lax.rem(wanted, capacity) == origin).astype(BF)

    def compact(expert, index, carry):
        columns = pl.ds(pl.multiple_of(index * step, step), step)
        out_ref[expert, :, columns] = jnp.dot(
            pick,
            arrived[:, expert, :, columns].reshape(n_node * PAD, step),
            preferred_element_type=F32,
        ).astype(BF)
        return carry

    for expert in range(2):
        lax.fori_loop(0, half // step, functools.partial(compact, expert), 0)

    for copy in first + second + third:
        copy.wait_send()

    @pl.when(core != lax.rem(x, 2))
    def _():
        for copy in swaps:
            copy.wait()


def wrap(p):
    return lax.rem(p + SIDE, SIDE)


def expert_kernel(
    own_ref,
    gate_hbm,
    up_hbm,
    down_hbm,
    gate_swap,
    up_swap,
    down_swap,
    out_ref,
    gate_ref,
    up_ref,
    down_ref,
    held,
    foreign,
    total,
    hidden,
    inner,
    r_half,
    r_full,
    x_recv,
    last,
    load_sem,
    ring_sem,
    cross_sem,
    chip_sem,
    r_ring_sem,
    r_cross_sem,
    r_chip_sem,
    last_sem,
):
    node, local = lax.axis_index("node"), lax.axis_index("local")
    core = lax.rem(node, 2)
    x, y = local // SIDE, lax.rem(local, SIDE)
    kind = lax.rem(x, 2)
    rows, width = held.shape[2], held.shape[3]
    half = width // 2
    units = hidden.shape[2]
    sibling = (node + 1 - 2 * core, local)

    def device(dx, dy):
        return (node, wrap(x + dx) * SIDE + wrap(y + dy))

    def blk(dx, dy):
        return wrap(x + dx) * SIDE + wrap(y + dy)

    greet([sibling, device(1, 0), device(-1, 0), device(2, 0), device(0, 1), device(0, -1)])

    wanted = (gate_ref, up_ref, down_ref)

    @pl.when(core == kind)
    def _():
        for index, source in enumerate((gate_hbm, up_hbm, down_hbm)):
            pltpu.make_async_copy(source.at[0], wanted[index], load_sem.at[index]).start()

    @pl.when(core != kind)
    def _():
        for index, source in enumerate((gate_swap, up_swap, down_swap)):
            pltpu.make_async_copy(source, wanted[index], load_sem.at[index]).start()

    def loaded(index):
        source = (gate_swap, up_swap, down_swap)[index]
        pltpu.make_async_copy(source, wanted[index], load_sem.at[index]).wait()

    def run(c):
        pending = {}

        def launch(key, copy):
            copy.start()
            pending.setdefault(key, []).append(copy)

        def settle(key):
            for copy in pending.pop(key, []):
                copy.wait_send()

        def key_of(dx, dy):
            return (dx % SIDE, dy % SIDE)

        held[c, blk(0, 0)] = own_ref[kind]
        foreign[wrap(y)] = own_ref[1 - kind]

        def chip_copy(cls, dx, dy):
            ref = held.at[cls, blk(dx, dy)]
            i = dx % SIDE * SIDE + dy % SIDE
            return remote(ref, ref, chip_sem.at[0, i], chip_sem.at[1, i], sibling)

        def share(dx, dy):
            launch(key_of(dx, dy), chip_copy(c, dx, dy))

        def slot(op, dy, columns):
            if c == 0:
                return held.at[0, blk(op, dy), :, columns], key_of(op, dy)
            if op == 0:
                return held.at[1, blk(0, dy), :, columns], key_of(0, dy)
            return foreign.at[wrap(y + dy), :, columns], ("F", dy % SIDE)

        def y_copy(op, way, dy, is_half):
            columns = pl.ds(way * half, half) if is_half else pl.ds(0, width)
            ref, key = slot(op, dy, columns)
            sem = 2 * is_half + way
            return key, remote(
                ref,
                ref,
                ring_sem.at[0, op, sem],
                ring_sem.at[1, op, sem],
                device(0, (1, -1)[way]),
            )

        def y_start(op):
            for way in range(2):
                launch(*y_copy(op, way, 0, False))

        def y_full_recv(op, way):
            dy = (-1, 1)[way]
            y_copy(op, way, dy, False)[1].wait_recv()
            launch(*y_copy(op, way, dy, True))

        def y_half_recv(op):
            for way in range(2):
                y_copy(op, way, 2, True)[1].wait_recv()

        def cross_send(dy):
            s = dy % SIDE
            there = held.at[c, blk(0, dy)]
            for way in range(2):
                launch(
                    ("F", s),
                    remote(
                        foreign.at[wrap(y + dy)],
                        there,
                        cross_sem.at[0, s, way],
                        cross_sem.at[1, s, way],
                        device((1, -1)[way], 0),
                    ),
                )
            launch(
                key_of(0, dy),
                remote(there, there, cross_sem.at[0, s, 2], cross_sem.at[1, s, 2], device(2, 0)),
            )

        def cross_recv(dy, way):
            s = dy % SIDE
            ref = held.at[c, blk((-1, 1, 2)[way], dy)]
            remote(
                ref, ref, cross_sem.at[0, s, way], cross_sem.at[1, s, way], device(2, 0)
            ).wait_recv()

        depth = 1280
        done = {}

        def unit(cls, block, ends):
            def body(index, carry):
                gate, upper = carry
                low = pl.multiple_of(index * depth, depth)
                deep = pl.ds(pl.multiple_of(cls * width + low, depth), depth)
                piece = held[cls, block, :, pl.ds(low, depth)]
                return (
                    gate + jnp.dot(piece, gate_ref[deep, :], preferred_element_type=F32),
                    upper + jnp.dot(piece, up_ref[deep, :], preferred_element_type=F32),
                )

            if ends:
                start = (total[block, :, 0:units], total[block, :, units : 2 * units])
            else:
                start = (jnp.zeros((rows, units), F32), jnp.zeros((rows, units), F32))
            gate, upper = lax.fori_loop(0, width // depth, body, start)
            if ends:
                hidden[block] = (jax.nn.silu(gate) * upper).astype(BF)
            else:
                total[block, :, 0:units] = gate
                total[block, :, units : 2 * units] = upper

        def compute(cls, places):
            if cls != c:
                for place in places:
                    chip_copy(cls, *place).wait_recv()
            for ends in (False, True):
                group = [p for p in places if (key_of(*p) in done) == ends]
                if not group:
                    continue

                def body(index, carry):
                    block = blk(*group[0])
                    for number in range(1, len(group)):
                        block = jnp.where(index == number, blk(*group[number]), block)
                    unit(cls, block, ends)
                    return carry

                if len(group) == 1:
                    body(0, 0)
                else:
                    lax.fori_loop(0, len(group), body, 0)
            for place in places:
                done[key_of(*place)] = True

        beside_y = [(0, -1), (0, 1)]
        if c == 0:
            cross_send(0)
            y_start(0)
            share(0, 0)
            loaded(0)
            loaded(1)
            compute(0, [(0, 0)])
            compute(1, [(0, 0)])
            for way in range(2):
                y_full_recv(0, way)
                share(*beside_y[way])
            compute(0, beside_y)
            compute(1, beside_y)
            for way, dx in enumerate((-1, 1, 2)):
                cross_recv(0, way)
                y_start(dx % SIDE)
                share(dx, 0)
            compute(0, [(-1, 0), (1, 0), (2, 0)])
            y_half_recv(0)
            share(0, 2)
            compute(1, [(-1, 0), (1, 0), (2, 0)])
            compute(0, [(0, 2)])
            compute(1, [(0, 2)])
            for dx in (-1, 1, 2):
                for way in range(2):
                    y_full_recv(dx % SIDE, way)
                    share(dx, (-1, 1)[way])
                compute(0, [(dx, -1), (dx, 1)])
                if dx != 2:
                    compute(1, [(-1, dx), (1, dx), (2, dx)])
            for dx in (-1, 1):
                y_half_recv(dx % SIDE)
                share(dx, 2)
                compute(0, [(dx, 2)])
            y_half_recv(2)
            share(2, 2)
            compute(0, [(2, 2)])
            compute(1, [(-1, 2), (1, 2), (2, 2)])
        else:
            y_start(0)
            y_start(1)
            cross_send(0)
            share(0, 0)
            loaded(0)
            loaded(1)
            compute(1, [(0, 0)])
            compute(0, [(0, 0)])
            for way in range(2):
                for op in range(2):
                    y_full_recv(op, way)
                cross_send((-1, 1)[way])
                share(*beside_y[way])
            compute(1, beside_y)
            compute(0, beside_y)
            for way, dx in enumerate((-1, 1, 2)):
                cross_recv(0, way)
                share(dx, 0)
            compute(1, [(-1, 0), (1, 0), (2, 0)])
            for op in range(2):
                y_half_recv(op)
            cross_send(2)
            share(0, 2)
            compute(0, [(-1, 0), (1, 0), (2, 0)])
            compute(1, [(0, 2)])
            compute(0, [(0, 2)])
            for dy in (-1, 1):
                for way, dx in enumerate((-1, 1, 2)):
                    cross_recv(dy, way)
                    share(dx, dy)
                compute(1, [(-1, dy), (1, dy), (2, dy)])
                compute(0, [(dy, -1), (dy, 1)])
            compute(0, [(2, -1), (2, 1)])
            compute(0, [(-1, 2), (1, 2)])
            for way, dx in enumerate((-1, 1, 2)):
                cross_recv(2, way)
                share(dx, 2)
            compute(1, [(-1, 2), (1, 2), (2, 2)])
            compute(0, [(2, 2)])

        loaded(2)
        step = 640

        def product(cls, block, dest, terms):
            for part in range(2):

                def body(index, carry):
                    low = pl.multiple_of(index * step, 128)
                    here = pl.multiple_of(low + part * half, 128)
                    columns = pl.ds(here, step)
                    value = None
                    if block is not None:
                        value = jnp.dot(
                            hidden[block],
                            down_ref[:, pl.ds(pl.multiple_of(here + cls * width, 128), step)],
                            preferred_element_type=F32,
                        )
                    for get, which in terms:
                        if which is None:
                            term = get(columns).astype(F32)
                        elif which == part:
                            term = get(pl.ds(low, step)).astype(F32)
                        else:
                            continue
                        value = term if value is None else value + term
                    dest[:, columns] = value.astype(BF)
                    return carry

                lax.fori_loop(0, half // step, body, 0)

        orders = (
            [(2, 2), (1, 2), (-1, 2), (0, 2), (2, 1), (2, -1), (1, 1), (1, -1), (2, 0)]
            + [(-1, 1), (-1, -1), (1, 0), (0, 1), (0, -1), (-1, 0), (0, 0)],
            [(2, 2), (1, 2), (-1, 2), (2, 1), (1, 1), (-1, 1), (0, 2), (2, -1), (1, -1)]
            + [(-1, -1), (0, 1), (2, 0), (1, 0), (-1, 0), (0, -1), (0, 0)],
        )
        queue = list(orders[1 - c])

        def inner_copy(cls, dx, dy):
            i = dx % SIDE * SIDE + dy % SIDE
            return remote(
                held.at[cls, blk(dx, dy)],
                inner.at[blk(dx, dy)],
                r_chip_sem.at[0, i],
                r_chip_sem.at[1, i],
                sibling,
            )

        def feed():
            if queue:
                dx, dy = queue.pop(0)
                block = blk(dx, dy)
                product(1 - c, block, held.at[1 - c, block], ())
                launch(("chip", dx, dy), inner_copy(1 - c, dx, dy))

        served = []

        def chip_sum(dx, dy, terms):
            served.append((dx, dy))
            block = blk(dx, dy)
            inner_copy(c, dx, dy).wait_recv()
            settle(key_of(dx, dy))
            product(
                c,
                block,
                held.at[c, block],
                [(lambda columns: inner[block, :, columns], None)] + terms,
            )
            feed()

        def ring_back(op, way, ref, is_half):
            if is_half:
                return remote(
                    ref.at[:, pl.ds(way * half, half)],
                    r_half.at[op, way],
                    r_ring_sem.at[0, op, way],
                    r_ring_sem.at[1, op, way],
                    device(0, (1, -1)[way]),
                )
            return remote(
                ref,
                r_full.at[op, way],
                r_ring_sem.at[0, op, 2 + way],
                r_ring_sem.at[1, op, 2 + way],
                device(0, (1, -1)[way]),
            )

        def half_term(op, way):
            ring_back(op, way, held.at[c, 0], True).wait_recv()
            return (lambda columns: r_half[op, way, :, columns], way)

        def full_terms(op):
            for way in range(2):
                ring_back(op, way, held.at[c, 0], False).wait_recv()
            return [
                (lambda columns: r_full[op, 0, :, columns], None),
                (lambda columns: r_full[op, 1, :, columns], None),
            ]

        def cross_back(s, way, ref):
            return remote(
                ref,
                x_recv.at[s, way],
                r_cross_sem.at[0, s, way],
                r_cross_sem.at[1, s, way],
                device((1, -1, 2)[way], 0),
            )

        def cross_term(s, way):
            cross_back(s, way, held.at[c, 0]).wait_recv()
            return (lambda columns: x_recv[s, way, :, columns], None)

        ours, theirs = held.at[c, blk(0, 0)], foreign.at[wrap(y)]
        feed()
        feed()
        if c == 0:

            def far(dx):
                chip_sum(dx, 2, [])
                for way in range(2):
                    launch("back", ring_back(dx % SIDE, way, held.at[0, blk(dx, 2)], True))

            def near(dx):
                for way in range(2):
                    dy = (1, -1)[way]
                    chip_sum(dx, dy, [half_term(dx % SIDE, way)])
                    launch("back", ring_back(dx % SIDE, way, held.at[0, blk(dx, dy)], False))

            def home(dx):
                terms = full_terms(dx % SIDE)
                if dx == 0:
                    terms.append(cross_term(0, 2))
                chip_sum(dx, 0, terms)
                if dx != 0:
                    way = {1: 0, -1: 1, 2: 2}[dx]
                    launch("back", cross_back(0, way, held.at[0, blk(dx, 0)]))

            for dx in (2, 1, -1, 0):
                far(dx)
            near(2)
            near(1)
            home(2)
            near(-1)
            home(1)
            near(0)
            home(-1)
            home(0)
            settle(("F", 0))
            product(0, None, theirs, [cross_term(0, 0), cross_term(0, 1)])
        else:

            def away(dy):
                for way, dx in ((2, 2), (0, 1), (1, -1)):
                    chip_sum(dx, dy, [])
                    launch("back", cross_back(dy % SIDE, way, held.at[1, blk(dx, dy)]))

            def home(dy):
                s = dy % SIDE
                extra = ([], [])
                for op in range(2):
                    if dy in (1, -1):
                        extra[op].append(half_term(op, (1, -1).index(dy)))
                    if dy == 0:
                        extra[op].extend(full_terms(op))
                chip_sum(0, dy, [cross_term(s, 2)] + extra[0])
                settle(("F", s))
                other = foreign.at[wrap(y + dy)]
                product(1, None, other, [cross_term(s, 0), cross_term(s, 1)] + extra[1])
                for op, ref in enumerate((held.at[1, blk(0, dy)], other)):
                    if dy == 2:
                        for way in range(2):
                            launch("back", ring_back(op, way, ref, True))
                    elif dy != 0:
                        launch("back", ring_back(op, (1, -1).index(dy), ref, False))

            away(2)
            away(1)
            home(2)
            away(-1)
            home(1)
            away(0)
            home(-1)
            home(0)
        assert served == orders[c] and not queue

        here, there = pl.ds(c * width, width), pl.ds((1 - c) * width, width)

        def finish(keep, give):
            copy = remote(give, last, last_sem.at[0], last_sem.at[1], sibling)
            copy.start()
            out_ref[:, here] = keep[...]
            copy.wait()

        @pl.when(kind == c)
        def _():
            finish(ours, theirs)

        @pl.when(kind != c)
        def _():
            finish(theirs, ours)

        out_ref[:, there] = last[...]
        for key in list(pending):
            settle(key)

    for c in range(2):
        pl.when(core == c)(functools.partial(run, c))


def on_device(n_node, n_local):
    def run(
        patches,
        norm_gain,
        vit_up,
        vit_down,
        adapter,
        text_rows,
        router,
        expert_ids,
        w_gate,
        w_up,
        w_down,
    ):
        vmem = pl.BlockSpec(memory_space=pltpu.VMEM)
        hbm = pl.BlockSpec(memory_space=pl.ANY)
        row_count, model = expert_ids.shape[0], adapter.shape[1]
        experts = router.shape[1]
        capacity = 7 * row_count // (8 * n_node)
        rows, width = patches.shape
        lanes = 128 * ((width // n_local + 127) // 128)
        own_rows = n_node * capacity
        units = w_gate.shape[2]
        half = model // 2
        swapped = [jax.ShapeDtypeStruct(w.shape[1:], BF) for w in (w_gate, w_up, w_down)]
        own, gate_swap, up_swap, down_swap = pl.pallas_call(
            functools.partial(vision_kernel, n_node, n_local, capacity),
            out_shape=[jax.ShapeDtypeStruct((2, own_rows, half), BF)] + swapped,
            in_specs=[vmem] * 8 + [hbm] * 3,
            out_specs=[vmem] + [hbm] * 3,
            scratch_shapes=[
                pltpu.VMEM((2, experts, PAD, half), BF),
                pltpu.VMEM((n_node, 2, PAD, half), BF),
                pltpu.VMEM((n_local, rows, lanes), BF),
                pltpu.VMEM((n_local, rows, lanes), BF),
                pltpu.VMEM((n_local, rows, lanes), BF),
                pltpu.VMEM((n_local, 2 * rows // n_local, half), BF),
                pltpu.VMEM((n_local, 2 * rows // n_local, half), BF),
                pltpu.SemaphoreType.DMA((4, n_local)),
                pltpu.SemaphoreType.DMA((2, n_node)),
                pltpu.SemaphoreType.DMA((2, 2, 3)),
            ],
            compiler_params=pltpu.CompilerParams(
                collective_id=0,
                has_side_effects=True,
                vmem_limit_bytes=48 * 2**20,
            ),
        )(
            patches,
            norm_gain.reshape(1, -1),
            vit_up,
            vit_down,
            adapter,
            text_rows,
            router,
            expert_ids,
            w_gate,
            w_up,
            w_down,
        )
        result = pl.pallas_call(
            expert_kernel,
            out_shape=jax.ShapeDtypeStruct((own_rows, model), BF),
            in_specs=[vmem] + [hbm] * 6,
            out_specs=vmem,
            scratch_shapes=[
                pltpu.VMEM((model, units), BF),
                pltpu.VMEM((model, units), BF),
                pltpu.VMEM((units, model), BF),
                pltpu.VMEM((2, n_local, own_rows, half), BF),
                pltpu.VMEM((SIDE, own_rows, half), BF),
                pltpu.VMEM((n_local, own_rows, 2 * units), F32),
                pltpu.VMEM((n_local, own_rows, units), BF),
                pltpu.VMEM((n_local, own_rows, half), BF),
                pltpu.VMEM((SIDE, 2, own_rows, half // 2), BF),
                pltpu.VMEM((SIDE, 2, own_rows, half), BF),
                pltpu.VMEM((SIDE, 3, own_rows, half), BF),
                pltpu.VMEM((own_rows, half), BF),
                pltpu.SemaphoreType.DMA((3,)),
                pltpu.SemaphoreType.DMA((2, SIDE, 4)),
                pltpu.SemaphoreType.DMA((2, SIDE, 3)),
                pltpu.SemaphoreType.DMA((2, n_local)),
                pltpu.SemaphoreType.DMA((2, SIDE, 4)),
                pltpu.SemaphoreType.DMA((2, SIDE, 3)),
                pltpu.SemaphoreType.DMA((2, n_local)),
                pltpu.SemaphoreType.DMA((2,)),
            ],
            compiler_params=pltpu.CompilerParams(
                collective_id=1,
                has_side_effects=True,
                vmem_limit_bytes=60 * 2**20,
            ),
        )(own, w_gate, w_up, w_down, gate_swap, up_swap, down_swap)
        return result[None]

    return run


def solution(mesh):
    in_specs = (
        P("node", None),
        P(),
        P(None, "local"),
        P("local", None),
        P("local", None),
        P(("node", "local"), None),
        P(),
        P(("node", "local"), None),
        P("node", None, "local"),
        P("node", None, "local"),
        P("node", "local", None),
    )
    out_specs = P("node", "local", None)
    return jax.shard_map(
        on_device(mesh.shape["node"], mesh.shape["local"]),
        mesh=mesh,
        in_specs=in_specs,
        out_specs=out_specs,
        check_vma=False,
    )
```

time: 271 us -> 260 us (0.959)
  Pallas kernels: 257 us -> 248 us
    pallas_call x2, Pallas kernels: 257 us -> 248 us  [the longest x1 149 us: run(): pl.pallas_call(expert_kernel, out_shape=jax.ShapeDtypeStruct((own_rows, m...]
    unnamed x16 -> x14, local copies, waits for them, and re-layouts: 10.1 us -> 10.9 us
where the time goes in v2:
time: 260 us; the launch traced here: 259 us
  Pallas kernels  248 us (95%)
  local copies, waits for them, and re-layouts  11.7 us (4%)
    pallas_call x1, Pallas kernels, run(): pl.pallas_call(expert_kernel, out_shape=jax.ShapeDtypeStruct((own_rows, m...  149 us
    pallas_call x1, Pallas kernels, run(): pl.pallas_call(functools.partial(vision_kernel, n_node, n_local, capacity...  98.5 us
    unnamed x14, local copies, waits for them, and re-layouts  10.9 us

profile of v2, /device:TPU:1, one launch (start us, length us, event | category | flops | bytes accessed | tf_op | source)
XLA Modules:
  0.0 259.4 jit_solution(13789283796368255401)
XLA Ops:
  0.0 0.0 copy-start
  0.0 0.0 copy-start.2
  0.0 0.9 reshape.3.gain_ref
  0.9 0.8 copy.14.ids_ref
  1.6 2.2 copy.12.up_ref
  3.8 2.5 copy.13.router_ref
  6.2 0.0 copy-done
  6.2 0.0 copy-done.2
  6.3 0.0 copy-start.3
  6.3 1.2 copy-done.3
  7.4 0.0 copy-start.4
  7.4 1.0 copy-done.4
  8.4 98.5 %shard_map.109 = (bf16[2,112,2560]{2,1,0:T(8,128)(2,1)S(1)}, bf16[5120,256]{1,0:T(8,128)(2,1)}, bf16[5120,256]{1,0:T(8,128)(2,1)}, bf16[256,5120]{1,0:T(8,128)(2,1)}) custom-call(bf16[128,1408]{1,0:T(8,128)(2,1)S(1)} %copy-done.4, f32[1,1408]{1,0:T(1,128)S(1)} %reshape.3.gain_ref, bf16[1408,352]{1,0:T(8,128)(2,1)S(1)} %copy.12.up_ref, ...), custom_call_target="tpu_custom_call" | custom-call | tf_op jit(solution)/shard_map/pallas_call | solution.py:787
  106.9 0.0 copy-start.1
  106.9 1.0 copy-done.1
  107.9 149.1 %shard_map.110 = bf16[112,5120]{1,0:T(8,128)(2,1)} custom-call(bf16[2,112,2560]{2,1,0:T(8,128)(2,1)} %copy-done.1, bf16[1,5120,256]{2,1,0:T(8,128)(2,1)} %gate_hbm.3, bf16[1,5120,256]{2,1,0:T(8,128)(2,1)} %up_hbm.3, bf16[1,256,5120]{2,1,0:T(8,128)(2,1)} %down_hbm.3, bf16[5120,256]{1,0:T(8,128)(2,1)} %get-tuple-element.10.gate_swap, ...), custom_call_target="tpu_custom_call" | custom-call | tf_op jit(solution)/shard_map/pallas_call | solution.py:822
  257.0 2.3 copy.16
Async XLA Ops:
  0.0 6.2 %copy-start = (bf16[120,5120]{1,0:T(8,128)(2,1)S(1)}, bf16[120,5120]{1,0:T(8,128)(2,1)}, u32[]{:S(2)}) copy-start(bf16[120,5120]{1,0:T(8,128)(2,1)} %text_ref.1) | copy-start | bytes 3686404
  0.0 6.2 %copy-start.2 = (bf16[352,1408]{1,0:T(8,128)(2,1)S(1)}, bf16[352,1408]{1,0:T(8,128)(2,1)}, u32[]{:S(2)}) copy-start(bf16[352,1408]{1,0:T(8,128)(2,1)} %down_ref.1) | copy-start | bytes 2973700
  6.3 1.2 copy-start.3
  7.4 1.0 copy-start.4
  106.9 1.0 copy-start.1

commit v3 on v2

--- a/solution.py
+++ b/solution.py
@@ -12,6 +12,7 @@
 F32 = jnp.float32
 SIDE = 4
 PAD = 16
+SWAP = (1, 3, 8)
 
 
 def remote(src, dst, send_sem, recv_sem, device):
@@ -36,23 +37,30 @@
     n_node,
     n_local,
     capacity,
+    share,
+    patches_hbm,
+    gain_ref,
+    vit_up_hbm,
+    vit_down_hbm,
+    adapter_hbm,
+    text_hbm,
+    router_ref,
+    ids_ref,
+    gate_hbm,
+    up_hbm,
+    out_ref,
+    gate_swap,
+    up_swap,
     patches_ref,
-    gain_ref,
     up_ref,
     down_ref,
     adapter_ref,
     text_ref,
-    router_ref,
-    ids_ref,
-    gate_hbm,
-    up_hbm,
-    down_hbm,
-    out_ref,
-    gate_swap,
-    up_swap,
-    down_swap,
+    load_sem,
     slots,
     arrived,
+    image_send,
+    image_recv,
     part_send,
     part_recv,
     patch_blocks,
@@ -69,48 +77,67 @@
     column = [(lax.rem(node + k, n_node), local) for k in range(1, n_node)]
     sibling = node + 1 - 2 * core
     beside = [(sibling, lax.rem(x + d, SIDE) * SIDE + y) for d in (SIDE - 1, 1)]
-    greet(peers + column + beside)
-
-    units = gate_hbm.shape[2]
+    loads = [
+        pltpu.make_async_copy(source, ref, load_sem.at[index])
+        for index, (source, ref) in enumerate(
+            (
+                (patches_hbm, patches_ref),
+                (vit_up_hbm, up_ref),
+                (vit_down_hbm, down_ref),
+                (text_hbm, text_ref),
+                (adapter_hbm, adapter_ref),
+            )
+        )
+    ]
+    for load in loads:
+        load.start()
+    barrier = pltpu.get_barrier_semaphore()
+    for device in peers + column + beside:
+        pl.semaphore_signal(barrier, inc=1, device_id=device, device_id_type=MESH)
+
+    units, model = gate_hbm.shape[2], gate_hbm.shape[1]
     swaps = []
-    for way in range(2):
-        part = pl.ds(way * (units // 2), units // 2)
-        for index, (here, there) in enumerate(
-            (
-                (gate_hbm.at[0, :, part], gate_swap.at[:, part]),
-                (up_hbm.at[0, :, part], up_swap.at[:, part]),
-                (down_hbm.at[0, part, :], down_swap.at[part, :]),
-            )
-        ):
-            swaps.append(
-                remote(
-                    here,
-                    there,
-                    swap_sem.at[0, way, index],
-                    swap_sem.at[1, way, index],
-                    beside[way],
+    for index, (here, there) in enumerate(((gate_hbm, gate_swap), (up_hbm, up_swap))):
+        for quarter in range(4):
+            deep = pl.ds(quarter * (model // 4), model // 4)
+            for way in range(2):
+                part = pl.ds(way * (units // 2), units // 2)
+                swaps.append(
+                    remote(
+                        here.at[0, deep, part],
+                        there.at[deep, part],
+                        swap_sem.at[0, way, index * 4 + quarter],
+                        swap_sem.at[1, way, index * 4 + quarter],
+                        beside[way],
+                    )
                 )
-            )
-
-    @pl.when(core != lax.rem(x, 2))
-    def _():
-        for copy in swaps:
-            copy.start()
+
+    def swap(low, high):
+        @pl.when(core != lax.rem(x, 2))
+        def _():
+            for copy in swaps[2 * low : 2 * high]:
+                copy.start()
 
     rows, width = patches_ref.shape
     block = width // n_local
+    loads[0].wait()
     values = patches_ref[...].astype(F32)
     center = jnp.mean(values, axis=-1, keepdims=True)
     spread = jnp.mean((values - center) ** 2, axis=-1, keepdims=True)
     normed = ((values - center) * lax.rsqrt(spread + 1e-05) * gain_ref[...]).astype(BF)
+    pl.semaphore_wait(barrier, len(peers + column + beside))
+    swap(0, SWAP[0])
+    last_dims = (((1,), (1,)), ((), ()))
+    loads[1].wait()
+    loads[2].wait()
     inner = jax.nn.gelu(
-        jnp.dot(normed, up_ref[...], preferred_element_type=F32), approximate=True
+        lax.dot_general(normed, up_ref[...], last_dims, preferred_element_type=F32),
+        approximate=True,
     ).astype(BF)
     partial_sum = jnp.dot(inner, down_ref[...], preferred_element_type=F32)
     for index in range(n_local):
         low = index * block
         part_send[index, :, 0:block] = partial_sum[:, low : low + block].astype(BF)
-        patch_blocks[index, :, 0:block] = values[:, low : low + block].astype(BF)
 
     first = []
     for k in range(1, n_local):
@@ -123,35 +150,39 @@
         )
         copy.start()
         first.append(copy)
-
-    text_rows, model = text_ref.shape
-    all_rows = ids_ref.shape[0]
-    experts = router_ref.shape[1]
-    chosen = ids_ref[...]
+    swap(SWAP[0], SWAP[1])
+
+    for index in range(n_local):
+        low = index * block
+        patch_blocks[index, :, 0:block] = values[:, low : low + block].astype(BF)
+    text_rows = text_ref.shape[0]
+    all_rows = ids_ref.shape[1]
+    experts = router_ref.shape[0]
+    square = (all_rows, all_rows)
+    chosen = jnp.transpose(jnp.broadcast_to(ids_ref[...].astype(F32), square))[:, 0:1]
     table = (
-        chosen == lax.broadcasted_iota(jnp.int32, (all_rows, experts), 1)
+        chosen == lax.broadcasted_iota(jnp.int32, (all_rows, experts), 1).astype(F32)
     ).astype(F32)
     earlier = (
-        lax.broadcasted_iota(jnp.int32, (all_rows, all_rows), 0)
-        > lax.broadcasted_iota(jnp.int32, (all_rows, all_rows), 1)
+        lax.broadcasted_iota(jnp.int32, square, 0) > lax.broadcasted_iota(jnp.int32, square, 1)
     ).astype(BF)
     counts = jnp.dot(earlier, table.astype(BF), preferred_element_type=F32)
-    rank = jnp.sum(counts * table, axis=1, keepdims=True).astype(jnp.int32)
-    slot = jnp.where(rank < capacity, chosen * PAD + rank, -1)
+    rank = jnp.sum(counts * table, axis=1, keepdims=True)
+    slot = jnp.where(rank < capacity, chosen * PAD + rank, -1.0).astype(jnp.int32)
     place = jnp.transpose(
         (slot == lax.broadcasted_iota(jnp.int32, (all_rows, experts * PAD), 1)).astype(F32)
     ).astype(BF)
-    logits = jnp.dot(text_ref[...], router_ref[...], preferred_element_type=F32)
-    score = jax.nn.sigmoid(
-        jnp.sum(logits * table[0:text_rows], axis=1, keepdims=True)
+    loads[3].wait()
+    logits = lax.dot_general(
+        text_ref[...], router_ref[...], last_dims, preferred_element_type=F32
     )
+    score = jax.nn.sigmoid(jnp.sum(logits * table[0:text_rows], axis=1, keepdims=True))
     step = 512
-
-    half = model // 2
+    shares = (share, model - share)
 
     def place_text(part, index, carry):
         low = pl.multiple_of(index * step, step)
-        columns = pl.ds(pl.multiple_of(part * half + low, step), step)
+        columns = pl.ds(pl.multiple_of(part * share + low, step), step)
         scaled = text_ref[:, columns].astype(F32) * score
         scaled = jnp.concatenate(
             [scaled, jnp.zeros((all_rows - text_rows, step), F32)], axis=0
@@ -162,7 +193,40 @@
         return carry
 
     for part in range(2):
-        lax.fori_loop(0, half // step, functools.partial(place_text, part), 0)
+        lax.fori_loop(0, shares[part] // step, functools.partial(place_text, part), 0)
+        for expert in range(experts):
+            slots[part, expert, :, share : share + all_rows] = place[
+                expert * PAD : (expert + 1) * PAD
+            ]
+
+    def to_column(source_of, there, sem):
+        copies = []
+        for k in range(1, n_node):
+            copy = remote(
+                source_of(column[k - 1][0]),
+                there.at[node],
+                node_sem.at[sem, k],
+                node_sem.at[sem + 1, k],
+                column[k - 1],
+            )
+            copy.start()
+            copies.append(copy)
+        mine = pltpu.make_async_copy(source_of(node), there.at[node], node_sem.at[sem, 0])
+        mine.start()
+
+        def arrive():
+            for k in range(1, n_node):
+                source = there.at[lax.rem(node + n_node - k, n_node)]
+                remote(
+                    source, source, node_sem.at[sem, k], node_sem.at[sem + 1, k], column[k - 1]
+                ).wait_recv()
+            mine.wait()
+
+        return copies, arrive
+
+    third, text_arrives = to_column(
+        lambda target: slots.at[lax.rem(target, 2), pl.ds(target // 2 * 2, 2)], arrived, 0
+    )
 
     total = part_send[local, :, 0:block].astype(F32)
     for k in range(1, n_local):
@@ -170,8 +234,11 @@
         total = total + part_recv[k, :, 0:block].astype(F32)
     vision = (patch_blocks[local, :, 0:block].astype(F32) + total).astype(BF)
 
+    half = model // 2
     own = rows // n_local
     wide = 640
+
+    loads[4].wait()
 
     def embed_part(index, carry):
         low = pl.ds(pl.multiple_of(index * wide, 128), wide)
@@ -197,6 +264,7 @@
         )
         copy.start()
         second.append(copy)
+    swap(SWAP[1], SWAP[2])
     for k in range(1, n_local):
         second[k - 1].wait_recv()
 
@@ -204,52 +272,32 @@
     for k in range(1, n_local):
         embed = embed + embed_recv[k].astype(F32)
     embed = embed.astype(BF).astype(F32)
-    image = jnp.dot(
-        embed[0:own].astype(BF), router_ref[0:half, :], preferred_element_type=F32
-    ) + jnp.dot(
-        embed[own : 2 * own].astype(BF), router_ref[half:model, :], preferred_element_type=F32
+    image = lax.dot_general(
+        embed[0:own].astype(BF), router_ref[:, 0:half], last_dims, preferred_element_type=F32
+    ) + lax.dot_general(
+        embed[own : 2 * own].astype(BF),
+        router_ref[:, half:model],
+        last_dims,
+        preferred_element_type=F32,
     )
     image_score = jax.nn.sigmoid(
         jnp.sum(image * table[text_rows:all_rows], axis=1, keepdims=True)
     )
+    scaled = jnp.concatenate([embed[0:own], embed[own : 2 * own]], axis=1) * image_score
     for part in range(2):
-        for low in range(0, half, step):
-            scaled = embed[part * own : (part + 1) * own, low : low + step] * image_score
-            scaled = jnp.concatenate(
-                [jnp.zeros((text_rows, step), F32), scaled], axis=0
-            ).astype(BF)
-            sent = jnp.dot(place, scaled, preferred_element_type=F32)
-            for expert in range(experts):
-                slots[part, expert, :, low : low + step] = (
-                    slots[part, expert, :, low : low + step].astype(F32)
-                    + sent[expert * PAD : (expert + 1) * PAD]
-                ).astype(BF)
-
-    third = []
-    for k in range(1, n_node):
-        target = column[k - 1][0]
-        copy = remote(
-            slots.at[lax.rem(target, 2), pl.ds(target // 2 * 2, 2)],
-            arrived.at[node],
-            node_sem.at[0, k],
-            node_sem.at[1, k],
-            column[k - 1],
-        )
-        copy.start()
-        third.append(copy)
-    mine = pltpu.make_async_copy(
-        slots.at[core, pl.ds(node // 2 * 2, 2)], arrived.at[node], node_sem.at[0, 0]
+        low, span = part * share, shares[part] // 2
+        image_send[part, :, 0:span] = jnp.concatenate(
+            [scaled[:, low : low + span], scaled[:, low + span : low + 2 * span]], axis=0
+        ).astype(BF)
+    fourth, image_arrives = to_column(
+        lambda target: image_send.at[lax.rem(target, 2)], image_recv, 2
     )
-    mine.start()
-    for k in range(1, n_node):
-        source = arrived.at[lax.rem(node + n_node - k, n_node)]
-        remote(source, source, node_sem.at[0, k], node_sem.at[1, k], column[k - 1]).wait_recv()
-    mine.wait()
 
     kept = out_ref.shape[1]
     wanted = lax.broadcasted_iota(jnp.int32, (kept, n_node * PAD), 0)
     origin = lax.broadcasted_iota(jnp.int32, (kept, n_node * PAD), 1)
     pick = (wanted // capacity * PAD + lax.rem(wanted, capacity) == origin).astype(BF)
+    text_arrives()
 
     def compact(expert, index, carry):
         columns = pl.ds(pl.multiple_of(index * step, step), step)
@@ -260,10 +308,49 @@
         ).astype(BF)
         return carry
 
+    row = lax.broadcasted_iota(jnp.int32, (all_rows, n_node * PAD), 0)
+    lane = lax.broadcasted_iota(jnp.int32, (all_rows, n_node * PAD), 1)
+    same = (wanted // capacity == origin // PAD).astype(F32)
+    spots = []
     for expert in range(2):
-        lax.fori_loop(0, half // step, functools.partial(compact, expert), 0)
-
-    for copy in first + second + third:
+        lax.fori_loop(0, share // step, functools.partial(compact, expert), 0)
+        places = jnp.dot(
+            pick,
+            arrived[:, expert, :, share : share + all_rows].reshape(n_node * PAD, all_rows),
+            preferred_element_type=F32,
+        ).astype(BF)
+        for top in range(2):
+            spread_rows = (
+                (row - text_rows + top * own == lax.rem(lane, PAD)) & (row >= text_rows)
+            ).astype(BF)
+            spot = jnp.dot(places, spread_rows, preferred_element_type=F32) * same
+            spots.append(spot.astype(BF))
+    image_arrives()
+
+    for c in range(2):
+
+        @pl.when(core == c)
+        def _(span=shares[c] // 2):
+            for expert in range(2):
+                for top in range(2):
+
+                    def add(index, carry):
+                        low = pl.multiple_of(index * step, step)
+                        columns = pl.ds(pl.multiple_of(top * span + low, step), step)
+                        image_rows = image_recv[:, :, pl.ds(low, step)]
+                        out_ref[expert, :, columns] = (
+                            out_ref[expert, :, columns].astype(F32)
+                            + jnp.dot(
+                                spots[2 * expert + top],
+                                image_rows.reshape(n_node * PAD, step),
+                                preferred_element_type=F32,
+                            )
+                        ).astype(BF)
+                        return carry
+
+                    lax.fori_loop(0, span // step, add, 0)
+
+    for copy in first + second + third + fourth:
         copy.wait_send()
 
     @pl.when(core != lax.rem(x, 2))
@@ -283,21 +370,24 @@
     down_hbm,
     gate_swap,
     up_swap,
-    down_swap,
     out_ref,
     gate_ref,
     up_ref,
     down_ref,
-    held,
-    foreign,
+    held0,
+    held1,
+    foreign0,
+    foreign1,
     total,
     hidden,
     inner,
     r_half,
     r_full,
-    x_recv,
+    x_recv0,
+    x_recv1,
     last,
     load_sem,
+    swap_sem,
     ring_sem,
     cross_sem,
     chip_sem,
@@ -310,8 +400,10 @@
     core = lax.rem(node, 2)
     x, y = local // SIDE, lax.rem(local, SIDE)
     kind = lax.rem(x, 2)
-    rows, width = held.shape[2], held.shape[3]
-    half = width // 2
+    held = (held0, held1)
+    widths = (held0.shape[2], held1.shape[2])
+    offsets = (0, widths[0])
+    rows = held0.shape[1]
     units = hidden.shape[2]
     sibling = (node + 1 - 2 * core, local)
 
@@ -321,26 +413,60 @@
     def blk(dx, dy):
         return wrap(x + dx) * SIDE + wrap(y + dy)
 
-    greet([sibling, device(1, 0), device(-1, 0), device(2, 0), device(0, 1), device(0, -1)])
-
-    wanted = (gate_ref, up_ref, down_ref)
+    beside = [(sibling[0], device(d, 0)[1]) for d in (-1, 1)]
+    greet(
+        [sibling, device(1, 0), device(-1, 0), device(2, 0), device(0, 1), device(0, -1)] + beside
+    )
+    downs = [
+        remote(
+            down_hbm.at[0, pl.ds(way * (units // 2), units // 2), :],
+            down_ref.at[pl.ds(way * (units // 2), units // 2), :],
+            swap_sem.at[0, way],
+            swap_sem.at[1, way],
+            beside[way],
+        )
+        for way in range(2)
+    ]
+    own_down = pltpu.make_async_copy(down_hbm.at[0], down_ref, load_sem.at[2])
 
     @pl.when(core == kind)
     def _():
-        for index, source in enumerate((gate_hbm, up_hbm, down_hbm)):
-            pltpu.make_async_copy(source.at[0], wanted[index], load_sem.at[index]).start()
+        for index, source in enumerate((gate_hbm, up_hbm)):
+            ref = (gate_ref, up_ref)[index]
+            pltpu.make_async_copy(source.at[0], ref, load_sem.at[index]).start()
+        own_down.start()
 
     @pl.when(core != kind)
     def _():
-        for index, source in enumerate((gate_swap, up_swap, down_swap)):
-            pltpu.make_async_copy(source, wanted[index], load_sem.at[index]).start()
+        for index, source in enumerate((gate_swap, up_swap)):
+            ref = (gate_ref, up_ref)[index]
+            pltpu.make_async_copy(source, ref, load_sem.at[index]).start()
 
     def loaded(index):
-        source = (gate_swap, up_swap, down_swap)[index]
-        pltpu.make_async_copy(source, wanted[index], load_sem.at[index]).wait()
+        if index < 2:
+            source, ref = ((gate_swap, gate_ref), (up_swap, up_ref))[index]
+            pltpu.make_async_copy(source, ref, load_sem.at[index]).wait()
+            return
+
+        @pl.when(core == kind)
+        def _():
+            own_down.wait()
+
+        @pl.when(core != kind)
+        def _():
+            for copy in downs:
+                copy.wait()
+
+    def swap_down():
+        @pl.when(core != kind)
+        def _():
+            for copy in downs:
+                copy.start()
 
     def run(c):
         pending = {}
+        width = widths[c]
+        half = width // 2
 
         def launch(key, copy):
             copy.start()
@@ -353,11 +479,22 @@
         def key_of(dx, dy):
             return (dx % SIDE, dy % SIDE)
 
-        held[c, blk(0, 0)] = own_ref[kind]
-        foreign[wrap(y)] = own_ref[1 - kind]
+        def foreign(dy):
+            return foreign0 if c == 0 else foreign1.at[wrap(y + dy)]
+
+        pieces = [
+            pltpu.make_async_copy(own_ref.at[index, :, pl.ds(0, width)], dest, load_sem.at[3 + n])
+            for n, (index, dest) in enumerate(
+                ((kind, held[c].at[blk(0, 0)]), (1 - kind, foreign(0)))
+            )
+        ]
+        for piece in pieces:
+            piece.start()
+        for piece in pieces:
+            piece.wait()
 
         def chip_copy(cls, dx, dy):
-            ref = held.at[cls, blk(dx, dy)]
+            ref = held[cls].at[blk(dx, dy)]
             i = dx % SIDE * SIDE + dy % SIDE
             return remote(ref, ref, chip_sem.at[0, i], chip_sem.at[1, i], sibling)
 
@@ -366,10 +503,10 @@
 
         def slot(op, dy, columns):
             if c == 0:
-                return held.at[0, blk(op, dy), :, columns], key_of(op, dy)
+                return held0.at[blk(op, dy), :, columns], key_of(op, dy)
             if op == 0:
-                return held.at[1, blk(0, dy), :, columns], key_of(0, dy)
-            return foreign.at[wrap(y + dy), :, columns], ("F", dy % SIDE)
+                return held1.at[blk(0, dy), :, columns], key_of(0, dy)
+            return foreign1.at[wrap(y + dy), :, columns], ("F", dy % SIDE)
 
         def y_copy(op, way, dy, is_half):
             columns = pl.ds(way * half, half) if is_half else pl.ds(0, width)
@@ -398,12 +535,12 @@
 
         def cross_send(dy):
             s = dy % SIDE
-            there = held.at[c, blk(0, dy)]
+            there = held[c].at[blk(0, dy)]
             for way in range(2):
                 launch(
                     ("F", s),
                     remote(
-                        foreign.at[wrap(y + dy)],
+                        foreign(dy),
                         there,
                         cross_sem.at[0, s, way],
                         cross_sem.at[1, s, way],
@@ -417,20 +554,21 @@
 
         def cross_recv(dy, way):
             s = dy % SIDE
-            ref = held.at[c, blk((-1, 1, 2)[way], dy)]
+            ref = held[c].at[blk((-1, 1, 2)[way], dy)]
             remote(
                 ref, ref, cross_sem.at[0, s, way], cross_sem.at[1, s, way], device(2, 0)
             ).wait_recv()
 
-        depth = 1280
         done = {}
 
         def unit(cls, block, ends):
+            depth = widths[cls] // 2
+
             def body(index, carry):
                 gate, upper = carry
                 low = pl.multiple_of(index * depth, depth)
-                deep = pl.ds(pl.multiple_of(cls * width + low, depth), depth)
-                piece = held[cls, block, :, pl.ds(low, depth)]
+                deep = pl.ds(pl.multiple_of(offsets[cls] + low, 128), depth)
+                piece = held[cls][block, :, pl.ds(low, depth)]
                 return (
                     gate + jnp.dot(piece, gate_ref[deep, :], preferred_element_type=F32),
                     upper + jnp.dot(piece, up_ref[deep, :], preferred_element_type=F32),
@@ -440,7 +578,7 @@
                 start = (total[block, :, 0:units], total[block, :, units : 2 * units])
             else:
                 start = (jnp.zeros((rows, units), F32), jnp.zeros((rows, units), F32))
-            gate, upper = lax.fori_loop(0, width // depth, body, start)
+            gate, upper = lax.fori_loop(0, 2, body, start)
             if ends:
                 hidden[block] = (jax.nn.silu(gate) * upper).astype(BF)
             else:
@@ -475,6 +613,7 @@
             cross_send(0)
             y_start(0)
             share(0, 0)
+            swap_down()
             loaded(0)
             loaded(1)
             compute(0, [(0, 0)])
@@ -514,6 +653,7 @@
             y_start(1)
             cross_send(0)
             share(0, 0)
+            swap_down()
             loaded(0)
             loaded(1)
             compute(1, [(0, 0)])
@@ -551,20 +691,21 @@
             compute(0, [(2, 2)])
 
         loaded(2)
-        step = 640
+        step = 512
 
         def product(cls, block, dest, terms):
+            span = widths[cls] // 2
             for part in range(2):
 
                 def body(index, carry):
                     low = pl.multiple_of(index * step, 128)
-                    here = pl.multiple_of(low + part * half, 128)
+                    here = pl.multiple_of(low + part * span, 128)
                     columns = pl.ds(here, step)
                     value = None
                     if block is not None:
                         value = jnp.dot(
                             hidden[block],
-                            down_ref[:, pl.ds(pl.multiple_of(here + cls * width, 128), step)],
+                            down_ref[:, pl.ds(pl.multiple_of(here + offsets[cls], 128), step)],
                             preferred_element_type=F32,
                         )
                     for get, which in terms:
@@ -578,7 +719,7 @@
                     dest[:, columns] = value.astype(BF)
                     return carry
 
-                lax.fori_loop(0, half // step, body, 0)
+                lax.fori_loop(0, span // step, body, 0)
 
         orders = (
             [(2, 2), (1, 2), (-1, 2), (0, 2), (2, 1), (2, -1), (1, 1), (1, -1), (2, 0)]
@@ -591,8 +732,8 @@
         def inner_copy(cls, dx, dy):
             i = dx % SIDE * SIDE + dy % SIDE
             return remote(
-                held.at[cls, blk(dx, dy)],
-                inner.at[blk(dx, dy)],
+                held[cls].at[blk(dx, dy)],
+                inner.at[blk(dx, dy), :, pl.ds(0, widths[cls])],
                 r_chip_sem.at[0, i],
                 r_chip_sem.at[1, i],
                 sibling,
@@ -602,7 +743,7 @@
             if queue:
                 dx, dy = queue.pop(0)
                 block = blk(dx, dy)
-                product(1 - c, block, held.at[1 - c, block], ())
+                product(1 - c, block, held[1 - c].at[block], ())
                 launch(("chip", dx, dy), inner_copy(1 - c, dx, dy))
 
         served = []
@@ -615,7 +756,7 @@
             product(
                 c,
                 block,
-                held.at[c, block],
+                held[c].at[block],
                 [(lambda columns: inner[block, :, columns], None)] + terms,
             )
             feed()
@@ -624,45 +765,48 @@
             if is_half:
                 return remote(
                     ref.at[:, pl.ds(way * half, half)],
-                    r_half.at[op, way],
+                    r_half.at[op, way, :, pl.ds(0, half)],
                     r_ring_sem.at[0, op, way],
                     r_ring_sem.at[1, op, way],
                     device(0, (1, -1)[way]),
                 )
             return remote(
                 ref,
-                r_full.at[op, way],
+                r_full.at[op, way, :, pl.ds(0, width)],
                 r_ring_sem.at[0, op, 2 + way],
                 r_ring_sem.at[1, op, 2 + way],
                 device(0, (1, -1)[way]),
             )
 
         def half_term(op, way):
-            ring_back(op, way, held.at[c, 0], True).wait_recv()
+            ring_back(op, way, held[c].at[0], True).wait_recv()
             return (lambda columns: r_half[op, way, :, columns], way)
 
         def full_terms(op):
             for way in range(2):
-                ring_back(op, way, held.at[c, 0], False).wait_recv()
+                ring_back(op, way, held[c].at[0], False).wait_recv()
             return [
                 (lambda columns: r_full[op, 0, :, columns], None),
                 (lambda columns: r_full[op, 1, :, columns], None),
             ]
 
+        def crossed(s, way):
+            return x_recv0.at[way] if c == 0 else x_recv1.at[s, way]
+
         def cross_back(s, way, ref):
             return remote(
                 ref,
-                x_recv.at[s, way],
+                crossed(s, way),
                 r_cross_sem.at[0, s, way],
                 r_cross_sem.at[1, s, way],
                 device((1, -1, 2)[way], 0),
             )
 
         def cross_term(s, way):
-            cross_back(s, way, held.at[c, 0]).wait_recv()
-            return (lambda columns: x_recv[s, way, :, columns], None)
-
-        ours, theirs = held.at[c, blk(0, 0)], foreign.at[wrap(y)]
+            cross_back(s, way, held[c].at[0]).wait_recv()
+            return (lambda columns: crossed(s, way)[:, columns], None)
+
+        ours, theirs = held[c].at[blk(0, 0)], foreign(0)
         feed()
         feed()
         if c == 0:
@@ -670,13 +814,13 @@
             def far(dx):
                 chip_sum(dx, 2, [])
                 for way in range(2):
-                    launch("back", ring_back(dx % SIDE, way, held.at[0, blk(dx, 2)], True))
+                    launch("back", ring_back(dx % SIDE, way, held0.at[blk(dx, 2)], True))
 
             def near(dx):
                 for way in range(2):
                     dy = (1, -1)[way]
                     chip_sum(dx, dy, [half_term(dx % SIDE, way)])
-                    launch("back", ring_back(dx % SIDE, way, held.at[0, blk(dx, dy)], False))
+                    launch("back", ring_back(dx % SIDE, way, held0.at[blk(dx, dy)], False))
 
             def home(dx):
                 terms = full_terms(dx % SIDE)
@@ -685,7 +829,7 @@
                 chip_sum(dx, 0, terms)
                 if dx != 0:
                     way = {1: 0, -1: 1, 2: 2}[dx]
-                    launch("back", cross_back(0, way, held.at[0, blk(dx, 0)]))
+                    launch("back", cross_back(0, way, held0.at[blk(dx, 0)]))
 
             for dx in (2, 1, -1, 0):
                 far(dx)
@@ -704,7 +848,7 @@
             def away(dy):
                 for way, dx in ((2, 2), (0, 1), (1, -1)):
                     chip_sum(dx, dy, [])
-                    launch("back", cross_back(dy % SIDE, way, held.at[1, blk(dx, dy)]))
+                    launch("back", cross_back(dy % SIDE, way, held1.at[blk(dx, dy)]))
 
             def home(dy):
                 s = dy % SIDE
@@ -716,9 +860,9 @@
                         extra[op].extend(full_terms(op))
                 chip_sum(0, dy, [cross_term(s, 2)] + extra[0])
                 settle(("F", s))
-                other = foreign.at[wrap(y + dy)]
+                other = foreign(dy)
                 product(1, None, other, [cross_term(s, 0), cross_term(s, 1)] + extra[1])
-                for op, ref in enumerate((held.at[1, blk(0, dy)], other)):
+                for op, ref in enumerate((held1.at[blk(0, dy)], other)):
                     if dy == 2:
                         for way in range(2):
                             launch("back", ring_back(op, way, ref, True))
@@ -735,13 +879,18 @@
             home(0)
         assert served == orders[c] and not queue
 
-        here, there = pl.ds(c * width, width), pl.ds((1 - c) * width, width)
+        here = pl.ds(offsets[c], width)
+        there = pl.ds(offsets[1 - c], widths[1 - c])
+        incoming = last.at[:, pl.ds(0, widths[1 - c])]
 
         def finish(keep, give):
-            copy = remote(give, last, last_sem.at[0], last_sem.at[1], sibling)
+            copy = remote(
+                give, last.at[:, pl.ds(0, width)], last_sem.at[0], last_sem.at[1], sibling
+            )
             copy.start()
             out_ref[:, here] = keep[...]
-            copy.wait()
+            remote(incoming, incoming, last_sem.at[0], last_sem.at[1], sibling).wait_recv()
+            copy.wait_send()
 
         @pl.when(kind == c)
         def _():
@@ -751,7 +900,7 @@
         def _():
             finish(theirs, ours)
 
-        out_ref[:, there] = last[...]
+        out_ref[:, there] = incoming[...]
         for key in list(pending):
             settle(key)
 
@@ -783,61 +932,74 @@
         own_rows = n_node * capacity
         units = w_gate.shape[2]
         half = model // 2
-        swapped = [jax.ShapeDtypeStruct(w.shape[1:], BF) for w in (w_gate, w_up, w_down)]
-        own, gate_swap, up_swap, down_swap = pl.pallas_call(
-            functools.partial(vision_kernel, n_node, n_local, capacity),
-            out_shape=[jax.ShapeDtypeStruct((2, own_rows, half), BF)] + swapped,
-            in_specs=[vmem] * 8 + [hbm] * 3,
-            out_specs=[vmem] + [hbm] * 3,
+        first = model * 3 // 5 // 512 * 512
+        second = model - first
+        swapped = [jax.ShapeDtypeStruct(w.shape[1:], BF) for w in (w_gate, w_up)]
+        own, gate_swap, up_swap = pl.pallas_call(
+            functools.partial(vision_kernel, n_node, n_local, capacity, first),
+            out_shape=[jax.ShapeDtypeStruct((2, own_rows, first), BF)] + swapped,
+            in_specs=[hbm, vmem, hbm, hbm, hbm, hbm, vmem, vmem] + [hbm] * 2,
+            out_specs=[vmem] + [hbm] * 2,
             scratch_shapes=[
-                pltpu.VMEM((2, experts, PAD, half), BF),
-                pltpu.VMEM((n_node, 2, PAD, half), BF),
+                pltpu.VMEM(patches.shape, BF),
+                pltpu.VMEM(vit_up.shape[::-1], BF),
+                pltpu.VMEM(vit_down.shape, BF),
+                pltpu.VMEM(adapter.shape, BF),
+                pltpu.VMEM(text_rows.shape, BF),
+                pltpu.SemaphoreType.DMA((5,)),
+                pltpu.VMEM((2, experts, PAD, first + row_count), BF),
+                pltpu.VMEM((n_node, 2, PAD, first + row_count), BF),
+                pltpu.VMEM((2, PAD, first // 2), BF),
+                pltpu.VMEM((n_node, PAD, first // 2), BF),
                 pltpu.VMEM((n_local, rows, lanes), BF),
                 pltpu.VMEM((n_local, rows, lanes), BF),
                 pltpu.VMEM((n_local, rows, lanes), BF),
                 pltpu.VMEM((n_local, 2 * rows // n_local, half), BF),
                 pltpu.VMEM((n_local, 2 * rows // n_local, half), BF),
                 pltpu.SemaphoreType.DMA((4, n_local)),
-                pltpu.SemaphoreType.DMA((2, n_node)),
-                pltpu.SemaphoreType.DMA((2, 2, 3)),
+                pltpu.SemaphoreType.DMA((4, n_node)),
+                pltpu.SemaphoreType.DMA((2, 2, 8)),
             ],
             compiler_params=pltpu.CompilerParams(
                 collective_id=0,
                 has_side_effects=True,
-                vmem_limit_bytes=48 * 2**20,
+                vmem_limit_bytes=63_000_000,
             ),
         )(
             patches,
             norm_gain.reshape(1, -1),
-            vit_up,
+            vit_up.T,
             vit_down,
             adapter,
             text_rows,
-            router,
-            expert_ids,
+            router.T,
+            expert_ids.reshape(1, -1),
             w_gate,
             w_up,
-            w_down,
         )
         result = pl.pallas_call(
             expert_kernel,
             out_shape=jax.ShapeDtypeStruct((own_rows, model), BF),
-            in_specs=[vmem] + [hbm] * 6,
+            in_specs=[hbm] * 6,
             out_specs=vmem,
             scratch_shapes=[
                 pltpu.VMEM((model, units), BF),
                 pltpu.VMEM((model, units), BF),
                 pltpu.VMEM((units, model), BF),
-                pltpu.VMEM((2, n_local, own_rows, half), BF),
-                pltpu.VMEM((SIDE, own_rows, half), BF),
+                pltpu.VMEM((n_local, own_rows, first), BF),
+                pltpu.VMEM((n_local, own_rows, second), BF),
+                pltpu.VMEM((own_rows, first), BF),
+                pltpu.VMEM((SIDE, own_rows, second), BF),
                 pltpu.VMEM((n_local, own_rows, 2 * units), F32),
                 pltpu.VMEM((n_local, own_rows, units), BF),
-                pltpu.VMEM((n_local, own_rows, half), BF),
-                pltpu.VMEM((SIDE, 2, own_rows, half // 2), BF),
-                pltpu.VMEM((SIDE, 2, own_rows, half), BF),
-                pltpu.VMEM((SIDE, 3, own_rows, half), BF),
-                pltpu.VMEM((own_rows, half), BF),
-                pltpu.SemaphoreType.DMA((3,)),
+                pltpu.VMEM((n_local, own_rows, first), BF),
+                pltpu.VMEM((SIDE, 2, own_rows, first // 2), BF),
+                pltpu.VMEM((SIDE, 2, own_rows, first), BF),
+                pltpu.VMEM((3, own_rows, first), BF),
+                pltpu.VMEM((SIDE, 3, own_rows, second), BF),
+                pltpu.VMEM((own_rows, first), BF),
+                pltpu.SemaphoreType.DMA((5,)),
+                pltpu.SemaphoreType.DMA((2, 2)),
                 pltpu.SemaphoreType.DMA((2, SIDE, 4)),
                 pltpu.SemaphoreType.DMA((2, SIDE, 3)),
                 pltpu.SemaphoreType.DMA((2, n_local)),
@@ -849,9 +1011,9 @@
             compiler_params=pltpu.CompilerParams(
                 collective_id=1,
                 has_side_effects=True,
-                vmem_limit_bytes=60 * 2**20,
+                vmem_limit_bytes=63_000_000,
             ),
-        )(own, w_gate, w_up, w_down, gate_swap, up_swap, down_swap)
+        )(own, w_gate, w_up, w_down, gate_swap, up_swap)
         return result[None]
 
     return run

time: 260 us -> 219 us (0.84)
  Pallas kernels: 248 us -> 214 us
  local copies, waits for them, and re-layouts: 11.7 us -> 3.63 us
    pallas_call x1, Pallas kernels: 98.5 us -> 60.5 us  [run(): pl.pallas_call(functools.partial(vision_kernel, n_node, n_local, capacity...]
    unnamed x14 -> x1, local copies, waits for them, and re-layouts: 10.9 us -> 2.34 us
    pallas_call x1, Pallas kernels: 149 us -> 153 us  [run(): pl.pallas_call(expert_kernel, out_shape=jax.ShapeDtypeStruct((own_rows, m...]
where the time goes in v3:
time: 219 us; the launch traced here: 217 us
  Pallas kernels  214 us (98%)
  local copies, waits for them, and re-layouts  3.63 us (2%)
    pallas_call x1, Pallas kernels, run(): pl.pallas_call(expert_kernel, out_shape=jax.ShapeDtypeStruct((own_rows, m...  153 us
    pallas_call x1, Pallas kernels, run(): pl.pallas_call(functools.partial(vision_kernel, n_node, n_local, capacity...  60.5 us

profile of v3, /device:TPU:1, one launch (start us, length us, event | category | flops | bytes accessed | tf_op | source)
XLA Modules:
  0.0 217.4 jit_solution(8757135165382179264)
XLA Ops:
  0.0 1.3 reshape.6.gain_ref
  1.3 60.5 %shard_map.109 = (bf16[2,112,3072]{2,1,0:T(8,128)(2,1)}, bf16[5120,256]{1,0:T(8,128)(2,1)}, bf16[5120,256]{1,0:T(8,128)(2,1)}) custom-call(bf16[128,1408]{1,0:T(8,128)(2,1)} %patches_hbm.1, f32[1,1408]{1,0:T(1,128)} %reshape.6.gain_ref, bf16[352,1408]{1,0:T(8,128)(2,1)} %bitcast.5, bf16[352,1408]{1,0:T(8,128)(2,1)} %vit_down_hbm.1, ...), custom_call_target="tpu_custom_call" | custom-call | tf_op jit(solution)/shard_map/pallas_call | solution.py:938
  61.8 153.2 %shard_map.110 = bf16[112,5120]{1,0:T(8,128)(2,1)} custom-call(bf16[2,112,3072]{2,1,0:T(8,128)(2,1)} %get-tuple-element.8.own_ref, bf16[1,5120,256]{2,1,0:T(8,128)(2,1)} %gate_hbm.3, bf16[1,5120,256]{2,1,0:T(8,128)(2,1)} %up_hbm.3, bf16[1,256,5120]{2,1,0:T(8,128)(2,1)} %down_hbm.1, bf16[5120,256]{1,0:T(8,128)(2,1)} %get-tuple-element.9.gate_swap, ...), custom_call_target="tpu_custom_call" | custom-call | tf_op jit(solution)/shard_map/pallas_call | solution.py:980
  215.1 2.3 %copy.13 = bf16[1,112,5120]{2,1,0:T(8,128)(2,1)} copy(bf16[1,112,5120]{2,1,0:T(8,128)(2,1)} %bitcast.4) | data formatting | bytes 2293760

commit v4 on v3

--- a/solution.py
+++ b/solution.py
@@ -12,7 +12,7 @@
 F32 = jnp.float32
 SIDE = 4
 PAD = 16
-SWAP = (1, 3, 8)
+SWAP = (1, 3, 5, 8)
 
 
 def remote(src, dst, send_sem, recv_sem, device):
@@ -66,6 +66,8 @@
     patch_blocks,
     embed_send,
     embed_recv,
+    embed_send2,
+    embed_recv2,
     sems,
     node_sem,
     swap_sem,
@@ -124,7 +126,7 @@
     values = patches_ref[...].astype(F32)
     center = jnp.mean(values, axis=-1, keepdims=True)
     spread = jnp.mean((values - center) ** 2, axis=-1, keepdims=True)
-    normed = ((values - center) * lax.rsqrt(spread + 1e-05) * gain_ref[...]).astype(BF)
+    normed = ((values - center) * lax.rsqrt(spread + 1e-05) * gain_ref[...].reshape(1, -1)).astype(BF)
     pl.semaphore_wait(barrier, len(peers + column + beside))
     swap(0, SWAP[0])
     last_dims = (((1,), (1,)), ((), ()))
@@ -246,31 +248,55 @@
         left = jnp.dot(vision, adapter_ref[:, low], preferred_element_type=F32)
         right = jnp.dot(vision, adapter_ref[:, high], preferred_element_type=F32)
         for j in range(n_local):
-            embed_send[j, :, low] = jnp.concatenate(
+            spot = jnp.where(core == 0, j, j % SIDE * SIDE + j // SIDE)
+            embed_send[spot, :, low] = jnp.concatenate(
                 [left[j * own : (j + 1) * own], right[j * own : (j + 1) * own]], axis=0
             ).astype(BF)
         return carry
 
     lax.fori_loop(0, half // wide, embed_part, 0)
 
+    p1, p2 = jnp.where(core == 0, x, y), jnp.where(core == 0, y, x)
+    s1, s2 = jnp.where(core == 0, SIDE, 1), jnp.where(core == 0, 1, SIDE)
     second = []
-    for k in range(1, n_local):
+    for d in range(1, SIDE):
+        q1 = lax.rem(p1 + d, SIDE)
         copy = remote(
-            embed_send.at[peers[k - 1][1]],
-            embed_recv.at[k],
-            sems.at[2, k],
-            sems.at[3, k],
-            peers[k - 1],
+            embed_send.at[pl.ds(q1 * SIDE, SIDE)],
+            embed_recv.at[d],
+            sems.at[2, d],
+            sems.at[3, d],
+            (node, q1 * s1 + p2 * s2),
         )
         copy.start()
         second.append(copy)
     swap(SWAP[1], SWAP[2])
-    for k in range(1, n_local):
-        second[k - 1].wait_recv()
-
-    embed = embed_send[local].astype(F32)
-    for k in range(1, n_local):
-        embed = embed + embed_recv[k].astype(F32)
+    for copy in second:
+        copy.wait_recv()
+
+    def ring_sum(q2):
+        value = embed_send[p1 * SIDE + q2].astype(F32)
+        for d in range(1, SIDE):
+            value = value + embed_recv[d, q2].astype(F32)
+        return value
+
+    for d in range(1, SIDE):
+        q2 = lax.rem(p2 + d, SIDE)
+        embed_send2[d] = ring_sum(q2).astype(BF)
+        copy = remote(
+            embed_send2.at[d],
+            embed_recv2.at[d],
+            sems.at[2, SIDE + d],
+            sems.at[3, SIDE + d],
+            (node, p1 * s1 + q2 * s2),
+        )
+        copy.start()
+        second.append(copy)
+    swap(SWAP[2], SWAP[3])
+    embed = ring_sum(p2)
+    for d in range(1, SIDE):
+        second[SIDE - 2 + d].wait_recv()
+        embed = embed + embed_recv2[d].astype(F32)
     embed = embed.astype(BF).astype(F32)
     image = lax.dot_general(
         embed[0:own].astype(BF), router_ref[:, 0:half], last_dims, preferred_element_type=F32
@@ -613,7 +639,6 @@
             cross_send(0)
             y_start(0)
             share(0, 0)
-            swap_down()
             loaded(0)
             loaded(1)
             compute(0, [(0, 0)])
@@ -627,6 +652,7 @@
                 cross_recv(0, way)
                 y_start(dx % SIDE)
                 share(dx, 0)
+            swap_down()
             compute(0, [(-1, 0), (1, 0), (2, 0)])
             y_half_recv(0)
             share(0, 2)
@@ -653,7 +679,6 @@
             y_start(1)
             cross_send(0)
             share(0, 0)
-            swap_down()
             loaded(0)
             loaded(1)
             compute(1, [(0, 0)])
@@ -672,6 +697,7 @@
             for op in range(2):
                 y_half_recv(op)
             cross_send(2)
+            swap_down()
             share(0, 2)
             compute(0, [(-1, 0), (1, 0), (2, 0)])
             compute(1, [(0, 2)])
@@ -955,7 +981,9 @@
                 pltpu.VMEM((n_local, rows, lanes), BF),
                 pltpu.VMEM((n_local, rows, lanes), BF),
                 pltpu.VMEM((n_local, 2 * rows // n_local, half), BF),
-                pltpu.VMEM((n_local, 2 * rows // n_local, half), BF),
+                pltpu.VMEM((SIDE, SIDE, 2 * rows // n_local, half), BF),
+                pltpu.VMEM((SIDE, 2 * rows // n_local, half), BF),
+                pltpu.VMEM((SIDE, 2 * rows // n_local, half), BF),
                 pltpu.SemaphoreType.DMA((4, n_local)),
                 pltpu.SemaphoreType.DMA((4, n_node)),
                 pltpu.SemaphoreType.DMA((2, 2, 8)),
@@ -967,7 +995,7 @@
             ),
         )(
             patches,
-            norm_gain.reshape(1, -1),
+            norm_gain,
             vit_up.T,
             vit_down,
             adapter,

time: 219 us -> 209 us (0.954)
  Pallas kernels: 214 us -> 207 us
    pallas_call x1, Pallas kernels: 60.5 us -> 56.3 us  [run(): pl.pallas_call(functools.partial(vision_kernel, n_node, n_local, capacity...]
    pallas_call x1, Pallas kernels: 153 us -> 150 us  [run(): pl.pallas_call(expert_kernel, out_shape=jax.ShapeDtypeStruct((own_rows, m...]
where the time goes in v4:
time: 209 us
  Pallas kernels  207 us (99%)
  local copies, waits for them, and re-layouts  2.34 us (1%)
    pallas_call x1, Pallas kernels, run(): pl.pallas_call(expert_kernel, out_shape=jax.ShapeDtypeStruct((own_rows, m...  150 us
    pallas_call x1, Pallas kernels, run(): pl.pallas_call(functools.partial(vision_kernel, n_node, n_local, capacity...  56.3 us

profile of v4, /device:TPU:1, one launch (start us, length us, event | category | flops | bytes accessed | tf_op | source)
XLA Modules:
  0.0 209.1 jit_solution(13772679480274177116)
XLA Ops:
  0.0 56.3 %shard_map.109 = (bf16[2,112,3072]{2,1,0:T(8,128)(2,1)}, bf16[5120,256]{1,0:T(8,128)(2,1)}, bf16[5120,256]{1,0:T(8,128)(2,1)}) custom-call(bf16[128,1408]{1,0:T(8,128)(2,1)} %patches_hbm.1, f32[1408]{0:T(1024)} %gain_ref.1, bf16[352,1408]{1,0:T(8,128)(2,1)} %bitcast.5, bf16[352,1408]{1,0:T(8,128)(2,1)} %vit_down_hbm.1, bf16[88,5120]{1,0:T(8,128)(2,1)} %adapter_hbm.1, ...), custom_call_target="tpu_custom_call" | custom-call | tf_op jit(solution)/shard_map/pallas_call | solution.py:964
  56.3 150.5 %shard_map.110 = bf16[112,5120]{1,0:T(8,128)(2,1)} custom-call(bf16[2,112,3072]{2,1,0:T(8,128)(2,1)} %get-tuple-element.8.own_ref, bf16[1,5120,256]{2,1,0:T(8,128)(2,1)} %gate_hbm.3, bf16[1,5120,256]{2,1,0:T(8,128)(2,1)} %up_hbm.3, bf16[1,256,5120]{2,1,0:T(8,128)(2,1)} %down_hbm.1, bf16[5120,256]{1,0:T(8,128)(2,1)} %get-tuple-element.9.gate_swap, ...), custom_call_target="tpu_custom_call" | custom-call | tf_op jit(solution)/shard_map/pallas_call | solution.py:1008
  206.7 2.3 %copy.13 = bf16[1,112,5120]{2,1,0:T(8,128)(2,1)} copy(bf16[1,112,5120]{2,1,0:T(8,128)(2,1)} %bitcast.4) | data formatting | bytes 2293760

commit v5 on v4

--- a/solution.py
+++ b/solution.py
@@ -12,7 +12,7 @@
 F32 = jnp.float32
 SIDE = 4
 PAD = 16
-SWAP = (1, 3, 5, 8)
+SWAP = (1, 3, 4, 8)
 
 
 def remote(src, dst, send_sem, recv_sem, device):
@@ -197,37 +197,59 @@
     for part in range(2):
         lax.fori_loop(0, shares[part] // step, functools.partial(place_text, part), 0)
         for expert in range(experts):
-            slots[part, expert, :, share : share + all_rows] = place[
+            slots[part, expert, :, shares[part] : shares[part] + all_rows] = place[
                 expert * PAD : (expert + 1) * PAD
             ]
 
-    def to_column(source_of, there, sem):
-        copies = []
-        for k in range(1, n_node):
-            copy = remote(
-                source_of(column[k - 1][0]),
-                there.at[node],
+    def to_column(source_of, there_of, sem):
+        def each(step_of):
+            for c in range(2):
+                pl.when(core == c)(functools.partial(step_of, c))
+
+        def copy_of(c, k):
+            cls = c if k % 2 == 0 else 1 - c
+            return remote(
+                source_of(cls, column[k - 1][0]),
+                there_of(cls, node),
                 node_sem.at[sem, k],
                 node_sem.at[sem + 1, k],
                 column[k - 1],
             )
-            copy.start()
-            copies.append(copy)
-        mine = pltpu.make_async_copy(source_of(node), there.at[node], node_sem.at[sem, 0])
-        mine.start()
-
-        def arrive():
+
+        def mine(c):
+            return pltpu.make_async_copy(
+                source_of(c, node), there_of(c, node), node_sem.at[sem, 0]
+            )
+
+        def begin(c):
             for k in range(1, n_node):
-                source = there.at[lax.rem(node + n_node - k, n_node)]
+                copy_of(c, k).start()
+            mine(c).start()
+
+        def arrive(c):
+            for k in range(1, n_node):
+                source = there_of(c, lax.rem(node + n_node - k, n_node))
                 remote(
                     source, source, node_sem.at[sem, k], node_sem.at[sem + 1, k], column[k - 1]
                 ).wait_recv()
-            mine.wait()
-
-        return copies, arrive
-
-    third, text_arrives = to_column(
-        lambda target: slots.at[lax.rem(target, 2), pl.ds(target // 2 * 2, 2)], arrived, 0
+            mine(c).wait()
+
+        def end(c):
+            for k in range(1, n_node):
+                copy_of(c, k).wait_send()
+
+        each(begin)
+        return functools.partial(each, arrive), functools.partial(each, end)
+
+    def first_lanes(ref, cls, extra):
+        return ref.at[:, :, pl.ds(0, shares[cls] + extra)]
+
+    text_arrives, text_ends = to_column(
+        lambda cls, target: first_lanes(
+            slots.at[cls, pl.ds(target // 2 * 2, 2)], cls, all_rows
+        ),
+        lambda cls, source: first_lanes(arrived.at[source], cls, all_rows),
+        0,
     )
 
     total = part_send[local, :, 0:block].astype(F32)
@@ -315,8 +337,10 @@
         image_send[part, :, 0:span] = jnp.concatenate(
             [scaled[:, low : low + span], scaled[:, low + span : low + 2 * span]], axis=0
         ).astype(BF)
-    fourth, image_arrives = to_column(
-        lambda target: image_send.at[lax.rem(target, 2)], image_recv, 2
+    image_arrives, image_ends = to_column(
+        lambda cls, target: image_send.at[cls, :, pl.ds(0, shares[cls] // 2)],
+        lambda cls, source: image_recv.at[source, :, pl.ds(0, shares[cls] // 2)],
+        2,
     )
 
     kept = out_ref.shape[1]
@@ -340,9 +364,10 @@
     spots = []
     for expert in range(2):
         lax.fori_loop(0, share // step, functools.partial(compact, expert), 0)
+        behind = pl.ds(pl.multiple_of(jnp.where(core == 0, shares[0], shares[1]), 128), all_rows)
         places = jnp.dot(
             pick,
-            arrived[:, expert, :, share : share + all_rows].reshape(n_node * PAD, all_rows),
+            arrived[:, expert, :, behind].reshape(n_node * PAD, all_rows),
             preferred_element_type=F32,
         ).astype(BF)
         for top in range(2):
@@ -376,8 +401,10 @@
 
                     lax.fori_loop(0, span // step, add, 0)
 
-    for copy in first + second + third + fourth:
+    for copy in first + second:
         copy.wait_send()
+    text_ends()
+    image_ends()
 
     @pl.when(core != lax.rem(x, 2))
     def _():
@@ -396,7 +423,8 @@
     down_hbm,
     gate_swap,
     up_swap,
-    out_ref,
+    out0_ref,
+    out1_ref,
     gate_ref,
     up_ref,
     down_ref,
@@ -440,9 +468,6 @@
         return wrap(x + dx) * SIDE + wrap(y + dy)
 
     beside = [(sibling[0], device(d, 0)[1]) for d in (-1, 1)]
-    greet(
-        [sibling, device(1, 0), device(-1, 0), device(2, 0), device(0, 1), device(0, -1)] + beside
-    )
     downs = [
         remote(
             down_hbm.at[0, pl.ds(way * (units // 2), units // 2), :],
@@ -455,6 +480,25 @@
     ]
     own_down = pltpu.make_async_copy(down_hbm.at[0], down_ref, load_sem.at[2])
 
+    def own_pieces(c):
+        places = (
+            (kind, held[c].at[blk(0, 0)]),
+            (1 - kind, foreign0 if c == 0 else foreign1.at[y]),
+        )
+        return [
+            pltpu.make_async_copy(
+                own_ref.at[index, :, pl.ds(0, widths[c])], dest, load_sem.at[3 + n]
+            )
+            for n, (index, dest) in enumerate(places)
+        ]
+
+    for c in range(2):
+
+        @pl.when(core == c)
+        def _():
+            for piece in own_pieces(c):
+                piece.start()
+
     @pl.when(core == kind)
     def _():
         for index, source in enumerate((gate_hbm, up_hbm)):
@@ -468,6 +512,10 @@
             ref = (gate_ref, up_ref)[index]
             pltpu.make_async_copy(source, ref, load_sem.at[index]).start()
 
+    greet(
+        [sibling, device(1, 0), device(-1, 0), device(2, 0), device(0, 1), device(0, -1)] + beside
+    )
+
     def loaded(index):
         if index < 2:
             source, ref = ((gate_swap, gate_ref), (up_swap, up_ref))[index]
@@ -508,15 +556,7 @@
         def foreign(dy):
             return foreign0 if c == 0 else foreign1.at[wrap(y + dy)]
 
-        pieces = [
-            pltpu.make_async_copy(own_ref.at[index, :, pl.ds(0, width)], dest, load_sem.at[3 + n])
-            for n, (index, dest) in enumerate(
-                ((kind, held[c].at[blk(0, 0)]), (1 - kind, foreign(0)))
-            )
-        ]
-        for piece in pieces:
-            piece.start()
-        for piece in pieces:
+        for piece in own_pieces(c):
             piece.wait()
 
         def chip_copy(cls, dx, dy):
@@ -717,10 +757,9 @@
             compute(0, [(2, 2)])
 
         loaded(2)
-        step = 512
-
         def product(cls, block, dest, terms):
             span = widths[cls] // 2
+            step = span // 2
             for part in range(2):
 
                 def body(index, carry):
@@ -905,8 +944,7 @@
             home(0)
         assert served == orders[c] and not queue
 
-        here = pl.ds(offsets[c], width)
-        there = pl.ds(offsets[1 - c], widths[1 - c])
+        outs = (out0_ref, out1_ref)
         incoming = last.at[:, pl.ds(0, widths[1 - c])]
 
         def finish(keep, give):
@@ -914,7 +952,7 @@
                 give, last.at[:, pl.ds(0, width)], last_sem.at[0], last_sem.at[1], sibling
             )
             copy.start()
-            out_ref[:, here] = keep[...]
+            outs[c][...] = keep[...]
             remote(incoming, incoming, last_sem.at[0], last_sem.at[1], sibling).wait_recv()
             copy.wait_send()
 
@@ -926,7 +964,7 @@
         def _():
             finish(theirs, ours)
 
-        out_ref[:, there] = incoming[...]
+        outs[1 - c][...] = incoming[...]
         for key in list(pending):
             settle(key)
 
@@ -991,7 +1029,7 @@
             compiler_params=pltpu.CompilerParams(
                 collective_id=0,
                 has_side_effects=True,
-                vmem_limit_bytes=63_000_000,
+                vmem_limit_bytes=63_400_000,
             ),
         )(
             patches,
@@ -1007,9 +1045,9 @@
         )
         result = pl.pallas_call(
             expert_kernel,
-            out_shape=jax.ShapeDtypeStruct((own_rows, model), BF),
+            out_shape=[jax.ShapeDtypeStruct((own_rows, size), BF) for size in (first, second)],
             in_specs=[hbm] * 6,
-            out_specs=vmem,
+            out_specs=[vmem] * 2,
             scratch_shapes=[
                 pltpu.VMEM((model, units), BF),
                 pltpu.VMEM((model, units), BF),
@@ -1039,10 +1077,10 @@
             compiler_params=pltpu.CompilerParams(
                 collective_id=1,
                 has_side_effects=True,
-                vmem_limit_bytes=63_000_000,
+                vmem_limit_bytes=63_400_000,
             ),
         )(own, w_gate, w_up, w_down, gate_swap, up_swap)
-        return result[None]
+        return jnp.concatenate(result, axis=1)[None]
 
     return run
 

time: 209 us -> 207 us (level)
  local copies, waits for them, and re-layouts: 2.34 us -> 0 us
  other arithmetic: 0 us -> 2.32 us
    unnamed x1 -> x0, local copies, waits for them, and re-layouts: 2.34 us -> none
    broadcast_in_dim x0 -> x1, other arithmetic: none -> 2.32 us  [run(): return jnp.concatenate(result, axis=1)[None]]
where the time goes in v5:
time: 207 us
  Pallas kernels  205 us (99%)
  other arithmetic  2.32 us (1%)
    pallas_call x1, Pallas kernels, run(): pl.pallas_call(expert_kernel, out_shape=[jax.ShapeDtypeStruct((own_rows,...  149 us
    pallas_call x1, Pallas kernels, run(): pl.pallas_call(functools.partial(vision_kernel, n_node, n_local, capacity...  55.8 us

profile of v5, /device:TPU:1, one launch (start us, length us, event | category | flops | bytes accessed | tf_op | source)
XLA Modules:
  0.0 207.1 jit_solution(4711535318566067414)
XLA Ops:
  0.0 55.8 %shard_map.109 = (bf16[2,112,3072]{2,1,0:T(8,128)(2,1)}, bf16[5120,256]{1,0:T(8,128)(2,1)}, bf16[5120,256]{1,0:T(8,128)(2,1)}) custom-call(bf16[128,1408]{1,0:T(8,128)(2,1)} %patches_hbm.1, f32[1408]{0:T(1024)} %gain_ref.1, bf16[352,1408]{1,0:T(8,128)(2,1)} %bitcast.5, bf16[352,1408]{1,0:T(8,128)(2,1)} %vit_down_hbm.1, bf16[88,5120]{1,0:T(8,128)(2,1)} %adapter_hbm.1, ...), custom_call_target="tpu_custom_call" | custom-call | tf_op jit(solution)/shard_map/pallas_call | solution.py:1002
  55.8 149.0 %shard_map.110 = (bf16[112,3072]{1,0:T(8,128)(2,1)}, bf16[112,2048]{1,0:T(8,128)(2,1)}) custom-call(bf16[2,112,3072]{2,1,0:T(8,128)(2,1)} %get-tuple-element.10.own_ref, bf16[1,5120,256]{2,1,0:T(8,128)(2,1)} %gate_hbm.3, bf16[1,5120,256]{2,1,0:T(8,128)(2,1)} %up_hbm.3, bf16[1,256,5120]{2,1,0:T(8,128)(2,1)} %down_hbm.1, ...), custom_call_target="tpu_custom_call" | custom-call | tf_op jit(solution)/shard_map/pallas_call | solution.py:1046
  204.8 2.3 %maximum_bitcast_fusion = bf16[1,112,5120]{2,1,0:T(8,128)(2,1)} fusion(bf16[112,2048]{1,0:T(8,128)(2,1)} %get-tuple-element.14, bf16[112,3072]{1,0:T(8,128)(2,1)} %get-tuple-element.13), kind=kLoop, calls=%fused_computation | loop fusion | flops 2293760 | bytes 2293760 | tf_op jit(solution)/shard_map/broadcast_in_dim | solution.py:1083

commit v6 on v5

--- a/solution.py
+++ b/solution.py
@@ -790,7 +790,7 @@
             [(2, 2), (1, 2), (-1, 2), (0, 2), (2, 1), (2, -1), (1, 1), (1, -1), (2, 0)]
             + [(-1, 1), (-1, -1), (1, 0), (0, 1), (0, -1), (-1, 0), (0, 0)],
             [(2, 2), (1, 2), (-1, 2), (2, 1), (1, 1), (-1, 1), (0, 2), (2, -1), (1, -1)]
-            + [(-1, -1), (0, 1), (2, 0), (1, 0), (-1, 0), (0, -1), (0, 0)],
+            + [(-1, -1), (2, 0), (1, 0), (-1, 0), (0, 1), (0, -1), (0, 0)],
         )
         queue = list(orders[1 - c])
 
@@ -938,8 +938,8 @@
             away(1)
             home(2)
             away(-1)
+            away(0)
             home(1)
-            away(0)
             home(-1)
             home(0)
         assert served == orders[c] and not queue

time: 207 us -> 204 us (0.986)
  Pallas kernels: 205 us -> 201 us
    pallas_call x1, Pallas kernels: 149 us -> 145 us  [run(): pl.pallas_call(expert_kernel, out_shape=[jax.ShapeDtypeStruct((own_rows,...]
where the time goes in v6:
time: 204 us; the launch traced here: 203 us
  Pallas kernels  201 us (99%)
  other arithmetic  2.32 us (1%)
    pallas_call x1, Pallas kernels, run(): pl.pallas_call(expert_kernel, out_shape=[jax.ShapeDtypeStruct((own_rows,...  145 us
    pallas_call x1, Pallas kernels, run(): pl.pallas_call(functools.partial(vision_kernel, n_node, n_local, capacity...  55.8 us

profile of v6, /device:TPU:1, one launch (start us, length us, event | category | flops | bytes accessed | tf_op | source)
XLA Modules:
  0.0 203.1 jit_solution(17748072105138699715)
XLA Ops:
  0.0 55.8 %shard_map.109 = (bf16[2,112,3072]{2,1,0:T(8,128)(2,1)}, bf16[5120,256]{1,0:T(8,128)(2,1)}, bf16[5120,256]{1,0:T(8,128)(2,1)}) custom-call(bf16[128,1408]{1,0:T(8,128)(2,1)} %patches_hbm.1, f32[1408]{0:T(1024)} %gain_ref.1, bf16[352,1408]{1,0:T(8,128)(2,1)} %bitcast.5, bf16[352,1408]{1,0:T(8,128)(2,1)} %vit_down_hbm.1, bf16[88,5120]{1,0:T(8,128)(2,1)} %adapter_hbm.1, ...), custom_call_target="tpu_custom_call" | custom-call | tf_op jit(solution)/shard_map/pallas_call | solution.py:1002
  55.8 145.0 %shard_map.110 = (bf16[112,3072]{1,0:T(8,128)(2,1)}, bf16[112,2048]{1,0:T(8,128)(2,1)}) custom-call(bf16[2,112,3072]{2,1,0:T(8,128)(2,1)} %get-tuple-element.10.own_ref, bf16[1,5120,256]{2,1,0:T(8,128)(2,1)} %gate_hbm.3, bf16[1,5120,256]{2,1,0:T(8,128)(2,1)} %up_hbm.3, bf16[1,256,5120]{2,1,0:T(8,128)(2,1)} %down_hbm.1, ...), custom_call_target="tpu_custom_call" | custom-call | tf_op jit(solution)/shard_map/pallas_call | solution.py:1046
  200.8 2.3 %maximum_bitcast_fusion = bf16[1,112,5120]{2,1,0:T(8,128)(2,1)} fusion(bf16[112,2048]{1,0:T(8,128)(2,1)} %get-tuple-element.14, bf16[112,3072]{1,0:T(8,128)(2,1)} %get-tuple-element.13), kind=kLoop, calls=%fused_computation | loop fusion | flops 2293760 | bytes 2293760 | tf_op jit(solution)/shard_map/broadcast_in_dim | solution.py:1083
